TPU v7x, 128 devices: a whole 4x4x4 slice. The times are simulated.
128 devices in a mesh: dom: 16 (over z, x), sub: 8 (over y, core).
Axes of the slice: x: 4, y: 4, z: 4, core: 2. Of those that a mesh axis runs over, the one named last changes fastest.
Arguments:
- positions: float32 [3, 4194304], P(None, ('dom', 'sub')), may hold values from -0.11 to 1.11
- velocities: float32 [3, 4194304], P(None, ('dom', 'sub')), may hold values from -3 to 3
- masses: float32 [4194304], P(('dom', 'sub')), may hold values from 0.003 to 0.012
- accel_prev: float32 [3, 4194304], P(None, ('dom', 'sub')), may hold values from -180 to 180
- active: int32 [4194304], P(('dom', 'sub')), may hold values from 0 to 1, as said below
- bucket_top: int32 [16384], P(('dom', 'sub')), may hold values from 0 to 4095
- near_list: int32 [16384, 4], P(('dom', 'sub')), may hold values from 0 to 1023, as said below
- cell_list: int32 [16384, 64], P(('dom', 'sub')), may hold values from 0 to 4095
- top_list: int32 [16384, 32], P(('dom', 'sub')), may hold values from 0 to 4095
- essential: int32 [16, 8, 16, 32], P('dom', 'sub'), may hold values from 0 to 1023
- work: int32 [5120], P(('dom', 'sub')), may hold values from 0 to 1023, as said below
Outputs:
- vel_out: float32 [3, 4194304], P(None, ('dom', 'sub'))
- pos_out: float32 [3, 4194304], P(None, ('dom', 'sub'))
Inputs may be any that keep to these rules, and one draw needn't show every extreme that they name: near_list[n, 0] is the group-local number of bucket n itself; every entry of row n names a bucket of n's group whose top cell differs from n's by at most one in each of the three top-cell coordinates. A bucket holds an active particle exactly when its group-local number appears in its group's block of work. `work`: entries g * 8 * 40 to (g + 1) * 8 * 40 - 1 are the block of domain group g and name distinct group-local buckets; in every group one device holds 128 of the named buckets.
All inputs are finite; a program needn't handle non-finite values.
Results may differ from a plain program's by a relative error of at most 0.0003.
Values sent between devices are 32-bit elements; how exact they have to be, the bound alone decides.
A program may use at most 64 MiB of HBM per device.

v0:
```python
import jax
import jax.numpy as jnp
from jax import lax
from jax.sharding import PartitionSpec as P

TOP_SIDE = 16
STEPS = 2
TOP = 4096


time_step = 0.01
soften = 0.0025
mass_floor = 0.5


def side_by_side(arrays, axis, dim, along):
    ends, at = ([], 0)
    for a in arrays[:-1]:
        at += a.shape[along]
        ends.append(at)
    both = jnp.concatenate(arrays, axis=along)
    return tuple(jnp.split(lax.all_gather(both, axis, axis=dim, tiled=True), ends, axis=along))


def rows_first(arrays, axis, dims):
    turned = [jnp.moveaxis(a, dim, 0) for a, dim in zip(arrays, dims)]
    both = jnp.concatenate([t.reshape(len(t), -1) for t in turned], axis=1)
    out, at, finished = (lax.all_gather(both, axis, axis=0, tiled=True), 0, [])
    for t, dim in zip(turned, dims):
        piece = out[:, at : at + t[0].size].reshape(-1, *t.shape[1:])
        finished.append(jnp.moveaxis(piece, 0, dim))
        at += t[0].size
    return tuple(finished)


def copy_for_each(x, axis):
    count = lax.axis_size(axis)
    return lax.all_to_all(jnp.broadcast_to(x[None], (count, *x.shape)), axis, 0, 0, tiled=True)


def laid_out(pieces, dim):
    pieces = jnp.moveaxis(pieces, 0, dim)
    shape = pieces.shape
    return pieces.reshape(*shape[:dim], shape[dim] * shape[dim + 1], *shape[dim + 2 :])


def collect(x, axis, dim):
    pieces = copy_for_each(x, axis)
    return laid_out(pieces, dim)


def in_blocks_2(x, dim, count):
    before, after = (x.shape[:dim], x.shape[dim + 1 :])
    return jnp.moveaxis(x.reshape(*before, count, -1, *after), dim, 0)


def summed_on_arrival(x, axis, dim):
    count = lax.axis_size(axis)
    pieces = lax.all_to_all(in_blocks_2(x, dim, count), axis, 0, 0, tiled=True)
    return jnp.sum(pieces, axis=0)


def taken_together(x, axis):
    everything = copy_for_each(x, axis)
    return jnp.sum(everything, axis=0)


def top_centres(top_ids):
    cell_side = TOP_SIDE
    first_index = top_ids // (cell_side * cell_side)
    second_index = top_ids // cell_side % cell_side
    third_index = top_ids % cell_side
    stacked = jnp.stack([first_index, second_index, third_index]).astype(jnp.float32)
    return (stacked + 0.5) / cell_side


def bucket_moments(places, weights):
    mass_total = jnp.sum(weights, axis=1)
    centre = jnp.sum(places * weights[None], axis=2) / mass_total[None]
    offsets = places - centre[:, :, None]
    radius_sq = jnp.sum(offsets * offsets, axis=0)

    def diagonal(first_axis):
        return jnp.sum(
            weights * (3.0 * offsets[first_axis] * offsets[first_axis] - radius_sq), axis=1
        )

    def crossed(first_axis, second_axis):
        return 3.0 * jnp.sum(weights * offsets[first_axis] * offsets[second_axis], axis=1)

    quadrupole = jnp.stack(
        [diagonal(0), diagonal(1), diagonal(2), crossed(0, 1), crossed(0, 2), crossed(1, 2)]
    )
    return jnp.concatenate([mass_total[None], centre, quadrupole], axis=0)


def top_raw(places, weights, centres):
    offsets = places - centres[:, :, None]
    weighted = weights[None] * offsets
    row_list = [
        weights,
        weighted[0],
        weighted[1],
        weighted[2],
        weighted[0] * offsets[0],
        weighted[1] * offsets[1],
        weighted[2] * offsets[2],
        weighted[0] * offsets[1],
        weighted[0] * offsets[2],
        weighted[1] * offsets[2],
    ]
    return jnp.stack([jnp.sum(row_values, axis=1) for row_values in row_list])


def top_moments(raw_sums, centres):
    mass_total = raw_sums[0]
    safe_mass = jnp.maximum(mass_total, mass_floor)
    first_sums = raw_sums[1:4]
    centre = centres + first_sums / safe_mass[None]
    cov_xx = raw_sums[4] - first_sums[0] * first_sums[0] / safe_mass
    cov_yy = raw_sums[5] - first_sums[1] * first_sums[1] / safe_mass
    cov_zz = raw_sums[6] - first_sums[2] * first_sums[2] / safe_mass
    cov_xy = raw_sums[7] - first_sums[0] * first_sums[1] / safe_mass
    cov_xz = raw_sums[8] - first_sums[0] * first_sums[2] / safe_mass
    cov_yz = raw_sums[9] - first_sums[1] * first_sums[2] / safe_mass
    trace_sum = cov_xx + cov_yy + cov_zz
    quadrupole = jnp.stack(
        [
            3.0 * cov_xx - trace_sum,
            3.0 * cov_yy - trace_sum,
            3.0 * cov_zz - trace_sum,
            3.0 * cov_xy,
            3.0 * cov_xz,
            3.0 * cov_yz,
        ]
    )
    return jnp.concatenate([mass_total[None], centre, quadrupole], axis=0)


def pair_accel(targets, sources, source_mass):
    offsets = sources[:, :, None] - targets[:, None, :]
    distance = jnp.sum(offsets * offsets, axis=0) + soften
    inverse = lax.rsqrt(distance)
    strength = source_mass[:, None] * inverse * inverse * inverse
    return jnp.sum(offsets * strength[None], axis=1)


def cell_accel(targets, moments):
    offsets = targets[:, None, :] - moments[1:4, :, None]
    distance = jnp.sum(offsets * offsets, axis=0) + soften
    inverse = lax.rsqrt(distance)
    inverse_sq = inverse * inverse
    inverse_three = inverse * inverse_sq
    inverse_five = inverse_three * inverse_sq
    inverse_seven = inverse_five * inverse_sq
    quadrupole = moments[4:10, :, None]
    along_x = quadrupole[0] * offsets[0] + quadrupole[3] * offsets[1] + quadrupole[4] * offsets[2]
    along_y = quadrupole[3] * offsets[0] + quadrupole[1] * offsets[1] + quadrupole[5] * offsets[2]
    along_z = quadrupole[4] * offsets[0] + quadrupole[5] * offsets[1] + quadrupole[2] * offsets[2]
    contracted = offsets[0] * along_x + offsets[1] * along_y + offsets[2] * along_z
    radial = -moments[0][:, None] * inverse_three - 2.5 * contracted * inverse_seven
    along_all = jnp.stack([along_x, along_y, along_z])
    return jnp.sum(offsets * radial[None] + along_all * inverse_five[None], axis=1)


def force_one(
    target, near_ids, cell_ids, top_ids, group_places, group_mass, essential_cells, top_cells
):
    sources = group_places[:, near_ids].reshape(3, -1)
    source_mass = group_mass[near_ids].reshape(-1)
    moments = jnp.concatenate(
        [jnp.take(essential_cells, cell_ids, axis=1), jnp.take(top_cells, top_ids, axis=1)], axis=1
    )
    return pair_accel(target, sources, source_mass) + cell_accel(target, moments)


def in_blocks(step_function, inputs, item_count):
    block_width = 4

    def reshape_leaf(values):
        return values.reshape((item_count // block_width, block_width) + values.shape[1:])

    result = lax.map(jax.vmap(step_function), jax.tree.map(reshape_leaf, inputs))
    return result.reshape((item_count,) + result.shape[2:])


def body(
    positions,
    velocities,
    masses,
    accel_prev,
    active,
    bucket_top,
    near_list,
    cell_list,
    top_list,
    essential,
    work,
):
    bucket_count = bucket_top.shape[0]
    bucket_size = positions.shape[1] // bucket_count
    sub_count = lax.axis_size("sub")
    dom_count = lax.axis_size("dom")
    sub_index = lax.axis_index("sub")
    group_buckets = sub_count * bucket_count
    activity = active.astype(jnp.float32)
    bucket_centres = top_centres(bucket_top)
    all_top_ids = jnp.arange(TOP, dtype=jnp.int32)
    placement = (bucket_top[:, None] == all_top_ids[None, :]).astype(jnp.float32)
    incoming = lax.all_to_all(
        essential.reshape(dom_count, -1), "dom", split_axis=0, concat_axis=0, tiled=True
    ).reshape(-1)
    shared_near, shared_cells, shared_tops, shared_work = (
        *side_by_side((near_list, cell_list, top_list), "sub", 0, 1),
        lax.all_gather(work, "sub", axis=0, tiled=True),
    )
    work_near = shared_near[work]
    work_cells = shared_cells[work]
    work_tops = shared_tops[work]
    own_ids = sub_index * bucket_count + jnp.arange(bucket_count, dtype=jnp.int32)
    matches = (own_ids[:, None] == shared_work[None, :]).astype(jnp.float32)
    places = positions
    speeds = velocities
    accel_now = accel_prev
    for substep in range(STEPS):
        half_speed = speeds + 0.5 * time_step * activity * accel_now
        places = places + time_step * half_speed
        group_places, group_mass = rows_first((places, masses), "sub", (1, 0))
        group_places = group_places.reshape(3, group_buckets, bucket_size)
        group_mass = group_mass.reshape(group_buckets, bucket_size)
        group_cells = bucket_moments(group_places, group_mass)
        replies = lax.all_to_all(
            jnp.take(group_cells, incoming, axis=1), "dom", split_axis=1, concat_axis=1, tiled=True
        )
        essential_cells = collect(replies, "sub", 1)
        own_places = places.reshape(3, bucket_count, bucket_size)
        own_mass = masses.reshape(bucket_count, bucket_size)
        spread_sums = jnp.dot(
            top_raw(own_places, own_mass, bucket_centres),
            placement,
            precision=lax.Precision.HIGHEST,
        )
        shares = summed_on_arrival(spread_sums, "sub", 1)
        shares = taken_together(shares, "dom")
        share_width = shares.shape[1]
        share_ids = sub_index * share_width + jnp.arange(share_width, dtype=jnp.int32)
        top_cells = collect(top_moments(shares, top_centres(share_ids)), "sub", 1)

        def one_bucket(work_item):
            target, near_ids, cell_ids, top_ids = work_item
            return force_one(
                target,
                near_ids,
                cell_ids,
                top_ids,
                group_places,
                group_mass,
                essential_cells,
                top_cells,
            )

        targets = jnp.transpose(group_places[:, work], (1, 0, 2))
        forces = in_blocks(one_bucket, (targets, work_near, work_cells, work_tops), work.shape[0])
        returned = collect(forces, "sub", 0)
        accel_own = jnp.einsum("bw,wcp->cbp", matches, returned, precision=lax.Precision.HIGHEST)
        accel_now = accel_own.reshape(3, -1)
        speeds = half_speed + 0.5 * time_step * activity * accel_now
    return (speeds, places)


def solution(mesh):
    in_specs = (
        P(None, ("dom", "sub")),
        P(None, ("dom", "sub")),
        P(("dom", "sub")),
        P(None, ("dom", "sub")),
        P(("dom", "sub")),
        P(("dom", "sub")),
        P(("dom", "sub"), None),
        P(("dom", "sub"), None),
        P(("dom", "sub"), None),
        P("dom", "sub", None, None),
        P(("dom", "sub")),
    )
    out_specs = (P(None, ("dom", "sub")), P(None, ("dom", "sub")))
    return jax.shard_map(body, mesh=mesh, in_specs=in_specs, out_specs=out_specs, check_vma=False)
```

profile of v0, /device:TPU:1, one launch (start us, length us, event | category | flops | bytes accessed | tf_op | source)
XLA Modules:
  0.0 716.4 jit_solution(3618833962155123418)
XLA Ops:
  11.8 8.5 %all-to-all-start = ((s32[16,1,32]{2,1,0:T(1,128)}), s32[16,1,32]{2,1,0:T(1,128)S(1)}, u32[]{:S(2)}, u32[]{:S(2)}) async-start(s32[16,1,32]{2,1,0:T(1,128)} %bitcast.60), calls=%async_computation | async-start | bytes 16384 | tf_op jit(solution)/shard_map/all_to_all | solution.py:210
  22.8 3.8 all-to-all-done
  26.6 6.6 all-to-all-start.3
  34.4 8.5 %all-to-all-done.3 = f32[8,10,512]{2,1,0:T(8,128)S(1)} async-done(((f32[8,10,512]{2,1,0:T(8,128)}), f32[8,10,512]{2,1,0:T(8,128)S(1)}, u32[]{:S(2)}, u32[]{:S(2)}) %all-to-all-start.3) | async-done | bytes 163872 | tf_op jit(solution)/shard_map/all_to_all | solution.py:59
  43.8 3.7 all-to-all-start.4
  48.1 9.8 %all-to-all-done.4 = f32[16,10,512]{2,1,0:T(8,128)S(1)} async-done(((f32[16,10,512]{2,1,0:T(8,128)}), f32[16,10,512]{2,1,0:T(8,128)S(1)}, u32[]{:S(2)}, u32[]{:S(2)}) %all-to-all-start.4) | async-done | bytes 327712 | tf_op jit(solution)/shard_map/all_to_all | solution.py:38
  58.6 12.5 %slice_reduce_fusion.1 = f32[262144]{0:T(1024)S(1)} fusion(f32[262144,4]{0,1:T(4,128)} %all-gather.3.cloned.1.call-done), kind=kLoop, calls=%fused_computation.178 | loop fusion | bytes 2097152 | tf_op jit(solution)/shard_map/slice | solution.py:30
  77.8 3.7 fusion.96
  82.8 12.0 %fusion.41 = f32[262144]{0:T(1024)} fusion(f32[3,262144]{1,0:T(4,128)S(1)} %bitcast.447, f32[262144,4]{0,1:T(4,128)S(1)} %copy-done.1), kind=kLoop, calls=%fused_computation.138 | loop fusion | flops 2097152 | bytes 7340032 | tf_op jit(solution)/shard_map/reduce_sum | solution.py:81
  103.9 4.6 concatenate.33
  116.5 5.6 all-to-all-done.1
  122.9 6.5 all-to-all-start.5
  136.7 4.4 all-to-all-start.2
  141.0 15.2 %all_gather.12 = s32[1024,100]{1,0:T(8,128)S(1)} all-gather(s32[128,100]{1,0:T(8,128)S(1)} %pad_add_fusion), channel_id=1, replica_groups=mesh['dom'=16,'sub'=8] {'sub'}, dimensions={0}, use_global_device_ids=true | all-gather | bytes 460800 | tf_op jit(solution)/shard_map/all_gather | solution.py:22
  167.1 191.3 %while.20 = (s32[]{:T(128)}, f32[10,4,3,256]{3,2,1,0:T(4,128)S(1)}, s32[10,4,4]{2,1,0:T(4,128)S(1)}, f32[3,1024,256]{2,0,1:T(4,128)}, f32[10,4,3,256]{3,1,2,0:T(...) while((s32[]{:T(128)}, f32[10,4,3,256]{3,2,1,0:T(4,128)S(1)}, ...), condition=%wide.region_26.30_spmd, body=%wide.region_21.29_spmd.sunk | while | flops 29599920 | bytes 26098504 | solution.py:183
  170.4 4.2 fusion.117
  189.5 4.2 fusion.117
  208.6 4.2 fusion.117
  227.7 4.2 fusion.117
  246.8 4.2 fusion.117
  265.9 4.2 fusion.117
  285.0 4.2 fusion.117
  304.1 4.2 fusion.117
  323.2 4.2 fusion.117
  342.3 4.2 fusion.117
  364.6 14.6 %all-reduce = s32[320]{0:T(512)S(1)} all-reduce(s32[320]{0:T(512)S(1)} %dynamic-update-slice), channel_id=1, replica_groups=mesh['dom'=16,'sub'=8] {'sub'}, use_global_device_ids=true, to_apply=%add | all-reduce | flops 320 | bytes 2560
  385.9 12.9 %all_to_all.78 = f32[8,10,512]{2,1,0:T(8,128)S(1)} all-to-all(f32[8,10,512]{2,1,0:T(8,128)S(1)} %bitcast.479), channel_id=1, replica_groups=mesh['dom'=16,'sub'=8] {'sub'}, dimensions={0} | all-to-all | bytes 327680 | tf_op jit(solution)/shard_map/all_to_all | solution.py:59
  398.9 12.9 %all_to_all.79 = f32[16,10,512]{2,1,0:T(8,128)S(1)} all-to-all(f32[16,10,512]{2,1,0:T(8,128)S(1)} %broadcast_in_dim.84), channel_id=1, replica_groups=mesh['dom'=16,'sub'=8] {'dom'}, dimensions={0} | all-to-all | bytes 655360 | tf_op jit(solution)/shard_map/all_to_all | solution.py:38
  411.9 4.0 all-gather.5.cloned.1.call-done
  415.9 12.5 %slice_reduce_fusion = f32[262144]{0:T(1024)S(1)} fusion(f32[262144,4]{0,1:T(4,128)} %all-gather.5.cloned.1.call-done), kind=kLoop, calls=%fused_computation.177 | loop fusion | bytes 2097152 | tf_op jit(solution)/shard_map/slice | solution.py:30
  436.9 11.1 %fusion.39 = f32[262144]{0:T(1024)S(1)} fusion(f32[3,262144]{1,0:T(4,128)S(1)} %bitcast.446, f32[262144,4]{0,1:T(4,128)S(1)} %copy-done), kind=kLoop, calls=%fused_computation.135 | loop fusion | flops 2097152 | bytes 7340032 | tf_op jit(solution)/shard_map/reduce_sum | solution.py:81
  453.6 4.6 all-to-all-start.7
  458.2 6.4 all-to-all-done.7
  465.4 5.0 all-to-all-start.11
  471.3 5.6 all-to-all-done.11
  477.7 5.3 all-to-all-start.8
  493.2 193.5 %while.21 = (s32[]{:T(128)}, f32[10,4,3,256]{3,2,1,0:T(4,128)}, s32[10,4,4]{2,1,0:T(4,128)S(1)}, f32[3,1024,256]{2,0,1:T(4,128)}, f32[10,4,3,256]{3,1,2,0:T(4,12...) while((s32[]{:T(128)}, f32[10,4,3,256]{3,2,1,0:T(4,128)}, ...), condition=%wide.region_52.56_spmd, body=%wide.region_47.55_spmd.sunk | while | flops 29599920 | bytes 27077504 | solution.py:183
  496.7 4.2 fusion.125
  516.1 4.2 fusion.125
  535.4 4.2 fusion.125
  554.8 4.2 fusion.125
  574.1 4.2 fusion.125
  593.4 4.2 fusion.125
  612.8 4.2 fusion.125
  632.1 4.2 fusion.125
  651.5 4.2 fusion.125
  670.9 4.2 fusion.125
  687.8 18.6 %all_to_all.77 = f32[8,40,3,256]{3,1,2,0:T(8,128)S(1)} all-to-all(f32[8,40,3,256]{3,1,2,0:T(8,128)S(1)} %broadcast_in_dim.87), channel_id=1, replica_groups=mesh['dom'=16,'sub'=8] {'sub'}, dimensions={0} | all-to-all | bytes 1966080 | tf_op jit(solution)/shard_map/all_to_all | solution.py:38
  (872 shorter events, 395.9 us)
Async XLA Ops:
  7.2 13.1 %copy-start.9 = (f32[32768]{0:T(1024)S(1)}, f32[32768]{0:T(1024)}, u32[]{:S(2)}) copy-start(f32[32768]{0:T(1024)} %param.23) | copy-start | bytes 393220
  7.2 13.3 %copy-start.21 = (s32[128]{0:T(128)S(1)}, s32[128]{0:T(128)}, u32[]{:S(2)}) copy-start(s32[128]{0:T(128)} %param.26) | copy-start | bytes 1540
  7.2 51.4 %all-gather.3.cloned.1.call-start = ((), (), s32[]{:S(2)}) async-start(), calls=%async_computation.13 | async-start | bytes 4718592 | tf_op jit(solution)/shard_map/all_gather | solution.py:28
  11.8 14.8 %all-to-all-start = ((s32[16,1,32]{2,1,0:T(1,128)}), s32[16,1,32]{2,1,0:T(1,128)S(1)}, u32[]{:S(2)}, u32[]{:S(2)}) async-start(s32[16,1,32]{2,1,0:T(1,128)} %bitcast.60), calls=%async_computation | async-start | bytes 16384 | tf_op jit(solution)/shard_map/all_to_all | solution.py:210
  20.4 14.0 %copy-start.17 = (f32[128]{0:T(128)}, f32[128]{0:T(128)S(1)}, u32[]{:S(2)}) copy-start(f32[128]{0:T(128)S(1)} %reduce_sum.459) | copy-start | bytes 1540
  26.6 16.3 %all-to-all-start.3 = ((f32[8,10,512]{2,1,0:T(8,128)}), f32[8,10,512]{2,1,0:T(8,128)S(1)}, u32[]{:S(2)}, u32[]{:S(2)}) async-start(f32[8,10,512]{2,1,0:T(8,128)} %bitcast.366), calls=%async_computation.3 | async-start | bytes 524288 | tf_op jit(solution)/shard_map/all_to_all | solution.py:59
  43.8 14.2 %all-to-all-start.4 = ((f32[16,10,512]{2,1,0:T(8,128)}), f32[16,10,512]{2,1,0:T(8,128)S(1)}, u32[]{:S(2)}, u32[]{:S(2)}) async-start(f32[16,10,512]{2,1,0:T(8,128)} %broadcast_in_dim.77), calls=%async_computation.4 | async-start | bytes 1048576 | tf_op jit(solution)/shard_map/all_to_all | solution.py:38
  72.6 3.9 copy-start.1
  101.8 28.3 %copy-start.15 = (s32[128,32]{0,1:T(8,128)S(1)}, s32[128,32]{0,1:T(8,128)}, u32[]{:S(2)}) copy-start(s32[128,32]{0,1:T(8,128)} %param.29) | copy-start | bytes 49156
  101.8 28.4 %copy-start.14 = (s32[128,64]{0,1:T(8,128)S(1)}, s32[128,64]{0,1:T(8,128)}, u32[]{:S(2)}) copy-start(s32[128,64]{0,1:T(8,128)} %param.28) | copy-start | bytes 98308
  112.3 9.9 %all-to-all-start.1 = ((f32[16,1,320]{2,1,0:T(1,128)}), f32[16,1,320]{2,1,0:T(1,128)S(1)}, u32[]{:S(2)}, u32[]{:S(2)}) async-start(f32[16,1,320]{2,1,0:T(1,128)} %reshape.1054), calls=%async_computation.1 | async-start | bytes 49152 | tf_op jit(solution)/shard_map/all_to_all | solution.py:232
  122.9 13.0 %all-to-all-start.5 = ((f32[8,10,512]{2,1,0:T(8,128)}), f32[8,10,512]{2,1,0:T(8,128)S(1)}, u32[]{:S(2)}, u32[]{:S(2)}) async-start(f32[8,10,512]{2,1,0:T(8,128)} %broadcast_in_dim.78), calls=%async_computation.5 | async-start | bytes 524288 | tf_op jit(solution)/shard_map/all_to_all | solution.py:38
  136.7 28.3 %all-to-all-start.2 = ((f32[8,10,512]{2,1,0:T(8,128)}), f32[8,10,512]{2,1,0:T(8,128)S(1)}, u32[]{:S(2)}, u32[]{:S(2)}) async-start(f32[8,10,512]{2,1,0:T(8,128)} %broadcast_in_dim.76), calls=%async_computation.2 | async-start | bytes 524288 | tf_op jit(solution)/shard_map/all_to_all | solution.py:38
  167.1 196.1 %copy-start.24 = (u32[128]{0:T(128)S(1)}, u32[128]{0:T(128)}, u32[]{:S(2)}) copy-start(u32[128]{0:T(128)} %constant.194) | copy-start | bytes 1540
  167.1 197.3 %copy-start.23 = (s32[40]{0:T(128)S(1)}, s32[40]{0:T(128)}, u32[]{:S(2)}) copy-start(s32[40]{0:T(128)} %param.31) | copy-start | bytes 484
  358.4 23.0 %copy-start.13 = (s32[10,4,32]{2,1,0:T(4,128)}, s32[10,4,32]{2,1,0:T(4,128)S(1)}, u32[]{:S(2)}) copy-start(s32[10,4,32]{2,1,0:T(4,128)S(1)} %get-tuple-element.640) | copy-start | bytes 15364
  358.4 23.0 %copy-start.2 = (f32[3,32768]{1,0:T(4,128)S(1)}, f32[3,32768]{1,0:T(4,128)}, u32[]{:S(2)}) copy-start(f32[3,32768]{1,0:T(4,128)} %param.22) | copy-start | bytes 1179652
  358.5 23.0 %copy-start.4 = (f32[3,32768]{1,0:T(4,128)S(1)}, f32[3,32768]{1,0:T(4,128)}, u32[]{:S(2)}) copy-start(f32[3,32768]{1,0:T(4,128)} %param.24) | copy-start | bytes 1179652
  359.5 19.8 %all-to-all-start.6 = ((f32[8,40,3,256]{3,1,2,0:T(8,128)}), f32[8,40,3,256]{3,1,2,0:T(8,128)S(1)}, u32[]{:S(2)}, u32[]{:S(2)}) async-start(f32[8,40,3,256]{3,1,2,0:T(8,128)} %broadcast_in_dim.80), calls=%async_computation.6 | async-start | bytes 1966080 | tf_op jit(solution)/shard_map/all_to_all | solution.py:38
  363.1 52.8 %all-gather.5.cloned.1.call-start = ((), (), s32[]{:S(2)}) async-start(), calls=%async_computation.14 | async-start | bytes 4718592 | tf_op jit(solution)/shard_map/all_gather | solution.py:28
  381.0 3.8 copy-start.18
  381.0 3.9 copy-start.22
  381.4 0.8 copy-start.7
  382.3 29.6 %copy-start.6 = (f32[3,32768]{1,0:T(4,128)}, f32[3,32768]{1,0:T(4,128)S(1)}, u32[]{:S(2)}) copy-start(f32[3,32768]{1,0:T(4,128)S(1)} %multiply_add_fusion.1) | copy-start | bytes 1179652
  428.9 3.5 copy-start
  447.9 4.6 copy-start.16
  453.6 11.1 %all-to-all-start.7 = ((f32[16,1,320]{2,1,0:T(1,128)}), f32[16,1,320]{2,1,0:T(1,128)S(1)}, u32[]{:S(2)}, u32[]{:S(2)}) async-start(f32[16,1,320]{2,1,0:T(1,128)} %reshape.1056), calls=%async_computation.7 | async-start | bytes 49152 | tf_op jit(solution)/shard_map/all_to_all | solution.py:232
  465.4 11.5 %all-to-all-start.11 = ((f32[8,10,512]{2,1,0:T(8,128)}), f32[8,10,512]{2,1,0:T(8,128)S(1)}, u32[]{:S(2)}, u32[]{:S(2)}) async-start(f32[8,10,512]{2,1,0:T(8,128)} %broadcast_in_dim.85), calls=%async_computation.11 | async-start | bytes 524288 | tf_op jit(solution)/shard_map/all_to_all | solution.py:38
  476.9 6.1 copy-start.10
  477.7 11.8 %all-to-all-start.8 = ((f32[8,10,512]{2,1,0:T(8,128)}), f32[8,10,512]{2,1,0:T(8,128)}, u32[]{:S(2)}, u32[]{:S(2)}) async-start(f32[8,10,512]{2,1,0:T(8,128)} %broadcast_in_dim.83), calls=%async_computation.8 | async-start | bytes 524288 | tf_op jit(solution)/shard_map/all_to_all | solution.py:38
  510.3 2.3 copy-start.12
  512.5 0.6 copy-start.11
  529.6 2.3 copy-start.12
  531.9 0.6 copy-start.11
  549.0 2.3 copy-start.12
  551.2 0.6 copy-start.11
  568.3 2.3 copy-start.12
  570.6 0.6 copy-start.11
  587.6 2.3 copy-start.12
  607.0 2.3 copy-start.12
  626.3 2.3 copy-start.12
  645.7 2.3 copy-start.12
  665.1 2.3 copy-start.12
  684.4 2.3 copy-start.12
  686.7 19.8 %copy-start.20 = (s32[128]{0:T(128)S(1)}, s32[128]{0:T(128)}, u32[]{:S(2)}) copy-start(s32[128]{0:T(128)} %copy-done.19) | copy-start | bytes 1540
  686.7 21.5 %copy-start.3 = (f32[3,32768]{1,0:T(4,128)S(1)}, f32[3,32768]{1,0:T(4,128)}, u32[]{:S(2)}) copy-start(f32[3,32768]{1,0:T(4,128)} %param.22) | copy-start | bytes 1179652
  686.7 21.5 %copy-start.5 = (f32[3,32768]{1,0:T(4,128)S(1)}, f32[3,32768]{1,0:T(4,128)}, u32[]{:S(2)}) copy-start(f32[3,32768]{1,0:T(4,128)} %param.24) | copy-start | bytes 1179652
  686.7 21.5 %copy-start.8 = (f32[1,3,128,256]{3,1,2,0:T(4,128)S(1)}, f32[1,3,128,256]{3,1,2,0:T(4,128)}, u32[]{:S(2)}) copy-start(f32[1,3,128,256]{3,1,2,0:T(4,128)} %copy-done.7) | copy-start | bytes 1179652
  (7 other events, 4.4 us)
Sparse Core Ops, SparseCore 0:
  11.9 38.5 all-gather.2
  384.5 31.3 all-gather.4
where the time goes:
time: 723 us; the launch traced here: 716 us
  other arithmetic  279 us (39%)
  local copies, waits for them, and re-layouts  242 us (33%)
  blocking collectives  74.1 us (10%)
  starting transfers between devices  51.6 us (7%)
  waiting for transfers between devices  47.4 us (7%)
  between operations  15.8 us (2%)
    reduce_sum x20, other arithmetic, pair_accel(): distance = jnp.sum(offsets * offsets, axis=0) + soften  83.4 us
    gather x20, local copies, waits for them, and re-layouts, force_one(): sources = group_places[:, near_ids].reshape(3, -1)  55.6 us
    mul x20, other arithmetic, pair_accel(): strength = source_mass[:, None] * inverse * inverse * inverse  53.3 us
    gather x40, local copies, waits for them, and re-layouts, force_one(): jnp.take(essential_cells, cell_ids, axis=1)  48.1 us
    reduce_sum x20, other arithmetic, pair_accel(): return jnp.sum(offsets * strength[None], axis=1)  39.3 us
    all_to_all x2, blocking collectives, copy_for_each(): lax.all_to_all(jnp.broadcast_to(x[None], (count, *x.shape)), axis, 0, 0,...  31.4 us
    gather x40, local copies, waits for them, and re-layouts, force_one(): jnp.take(top_cells, top_ids, axis=1)  30.7 us
    all_to_all x6, starting transfers between devices, copy_for_each(): lax.all_to_all(jnp.broadcast_to(x[None], (count, *x.shape)), axis, 0, 0,...  28.5 us
  transfers between devices with their start and end apart: 12, of which 9 were waited for; matrix products, arithmetic and copies ran while one was open for 4% of the time, Pallas kernels for 0%

commit v1 on v0

v1 whole, which is shorter than its diff:
```python
import jax
import jax.numpy as jnp
from jax import lax
from jax.experimental import pallas as pl
from jax.experimental.pallas import tpu as pltpu
from jax.sharding import PartitionSpec as P

f32, bf16, i32 = jnp.float32, jnp.bfloat16, jnp.int32
MESH = pl.DeviceIdType.MESH
SUB, DOM = 8, 16
BUCKETS, WIDE, ITEMS = 128, 256, 40
GROUP = SUB * BUCKETS
TOP_SIDE = 16
MIB = 2**20

time_step = 0.01
soften = 0.0025
mass_floor = 0.5
kick = 0.5 * time_step


def rnd(a):
    return a.astype(bf16).astype(f32)


def split3(a):
    h = rnd(a)
    r = a - h
    m = rnd(r)
    return h, m, rnd(r - m)


def dot(a, b, dims):
    return lax.dot_general(
        a.astype(bf16), b.astype(bf16), ((dims[:1], dims[1:]), ((), ())), preferred_element_type=f32
    )


def row_iota(shape):
    return lax.broadcasted_iota(i32, shape, 0)


def pick(rows, shape):
    at = row_iota(shape)
    out = jnp.zeros(shape, f32)
    for i, v in rows.items():
        out = jnp.where(at == i, v, out)
    return out


def square(y):
    q = y * y
    return q[0:1] + q[1:2] + q[2:3]


def moments(dense, top_row, rec_ref):
    first = [dense[c][:, 0:1] for c in range(3)]
    y = [dense[c] - first[c] for c in range(3)]
    m = dense[3]
    ones = jnp.ones((8, WIDE), f32)
    lead = jnp.where(lax.broadcasted_iota(i32, (8, WIDE), 1) == 0, 1.0, 0.0)

    def total(a, by=ones):
        return lax.dot_general(
            by, a, (((1,), (1,)), ((), ())), precision=lax.Precision.HIGHEST, preferred_element_type=f32
        )[0:1]

    my = [m * y[c] for c in range(3)]
    mass = total(m)
    start = [total(dense[c], lead) for c in range(3)]
    s = [total(my[c]) for c in range(3)]
    d = [s[c] / mass for c in range(3)]
    pairs = ((0, 0), (1, 1), (2, 2), (0, 1), (0, 2), (1, 2))
    second = [total(my[a] * y[b]) - s[a] * d[b] for a, b in pairs]
    rows = {0: mass, 10: top_row}
    for c in range(3):
        rows[1 + c] = start[c] + d[c]
    for k in range(6):
        rows[4 + k] = second[k]
    rec_ref[...] = pick(rows, (16, BUCKETS))


def first_kernel(pos, vel, acc, act, mass, top_row, half_ref, x4_ref, p4_ref, rec_ref, dense):
    def one(b, carry):
        sl = pl.ds(pl.multiple_of(b * WIDE, WIDE), WIDE)
        a = act[:, sl].astype(f32)
        h = vel[:, sl] + kick * a * acc[:, sl]
        x = pos[:, sl] + time_step * h
        half_ref[:, sl] = h
        m = mass[:, sl]
        x4_ref[b] = jnp.concatenate([x, m], axis=0)
        p4_ref[b] = jnp.concatenate([x + time_step * h, a], axis=0)
        for c in range(3):
            dense[c, pl.ds(b, 1), :] = x[c : c + 1]
        dense[3, pl.ds(b, 1), :] = m
        return carry

    lax.fori_loop(0, BUCKETS, one, 0, unroll=4)
    moments(dense, top_row[...], rec_ref)


def second_kernel(slot, x4, half, act, mass, top_row, force, half_ref, pos_ref, rec_ref, dense):
    def one(b, carry):
        sl = pl.ds(pl.multiple_of(b * WIDE, WIDE), WIDE)
        a = act[:, sl].astype(f32)
        f = jnp.where(slot[b] >= 0, force[jnp.maximum(slot[b], 0)][0:3], 0.0)
        push = kick * a * f
        h = half[:, sl] + push + push
        x = x4[b][0:3] + time_step * h
        half_ref[:, sl] = h
        pos_ref[:, sl] = x
        for c in range(3):
            dense[c, pl.ds(b, 1), :] = x[c : c + 1]
        dense[3, pl.ds(b, 1), :] = mass[:, sl]
        return carry

    lax.fori_loop(0, BUCKETS, one, 0, unroll=4)
    moments(dense, top_row[...], rec_ref)


def last_kernel(slot, half, act, force, vel_ref):
    def one(b, carry):
        sl = pl.ds(pl.multiple_of(b * WIDE, WIDE), WIDE)
        f = jnp.where(slot[b] >= 0, force[jnp.maximum(slot[b], 0)][0:3], 0.0)
        vel_ref[:, sl] = half[:, sl] + kick * act[:, sl].astype(f32) * f
        return carry

    lax.fori_loop(0, BUCKETS, one, 0, unroll=4)


def centre(ids):
    return [
        (part.astype(f32) + 0.5) / TOP_SIDE
        for part in (ids >> 8, (ids >> 4) & 15, ids & 15)
    ]


def cells_kernel(rec, out, top, part, sums, s1, r1, s2, r2, s3, r3, s4, r4):
    g, s = lax.axis_index("dom"), lax.axis_index("sub")
    across = [(lax.rem(g + k, DOM), s) for k in range(1, DOM)]
    within = [(g, lax.rem(s + k, SUB)) for k in range(1, SUB)]
    barrier = pltpu.get_barrier_semaphore()
    for peer in across + within:
        pl.semaphore_signal(barrier, inc=1, device_id=peer, device_id_type=MESH)
    pl.semaphore_wait(barrier, DOM + SUB - 2)

    def send(ref_from, ref_to, peers, sends, recvs):
        copies = [
            pltpu.make_async_remote_copy(
                src_ref=ref_from, dst_ref=ref_to, send_sem=sends.at[k], recv_sem=recvs.at[k],
                device_id=peer, device_id_type=MESH,
            )
            for k, peer in enumerate(peers)
        ]
        for c in copies:
            c.start()
        return copies

    def done(copies):
        for c in copies:
            c.wait()

    out[s, g] = rec[...]
    done(send(rec, out.at[s, g], across, s1, r1))
    done(send(out.at[s], out.at[s], within, s2, r2))

    base = (s * DOM + g) * 32
    ids = lax.broadcasted_iota(i32, (32, BUCKETS), 0) + base

    def values(t):
        mass = t[0:1]
        own = t[10:11].astype(i32)
        d = [t[1 + c : 2 + c] - at for c, at in enumerate(centre(own))]
        md = [mass * d[c] for c in range(3)]
        rows = {0: mass, 1: md[0], 2: md[1], 3: md[2]}
        for k, (a, b) in enumerate(((0, 0), (1, 1), (2, 2), (0, 1), (0, 2), (1, 2))):
            rows[4 + k] = t[4 + k : 5 + k] + md[a] * d[b]
        pieces = jnp.concatenate(split3(pick(rows, (16, BUCKETS))), axis=0)
        return pieces, jnp.where(ids == own, 1.0, 0.0)

    sums[...] = jnp.zeros_like(sums)

    def step(i, carry):
        row, k = i // 4, (i % 4) * 4
        got = [values(out[row, k + u]) for u in range(4)]
        v = jnp.concatenate([a for a, _ in got], axis=1)
        o = jnp.concatenate([b for _, b in got], axis=1)
        sums[...] += dot(v, o, (1, 1))
        return carry

    lax.fori_loop(0, SUB * DOM // 4, step, 0)
    t = sums[0:16] + sums[16:32] + sums[32:48]
    mass = t[0:1]
    w = jnp.maximum(mass, mass_floor)
    at = centre(lax.broadcasted_iota(i32, (1, 32), 1) + base)
    u = [t[1 + c : 2 + c] / w for c in range(3)]
    rows = {0: mass}
    for c in range(3):
        rows[1 + c] = at[c] + u[c]
    for k, (a, b) in enumerate(((0, 0), (1, 1), (2, 2), (0, 1), (0, 2), (1, 2))):
        rows[4 + k] = t[4 + k : 5 + k] - t[1 + a : 2 + a] * u[b]
    mine = pick(rows, (16, 32))
    four = jnp.concatenate([mine] * 4, axis=1)
    lane = lax.broadcasted_iota(i32, (16, 128), 1)
    part[g] = jnp.where(lane // 32 == lax.rem(g, 4), four, 0.0)
    done(send(part.at[g], part.at[g], across, s3, r3))
    for k in range(4):
        top[s, k] = part[4 * k] + part[4 * k + 1] + part[4 * k + 2] + part[4 * k + 3]
    done(send(top.at[s], top.at[s], within, s4, r4))


def spread(table, pieces, rows):
    at = row_iota((16, 128))
    extra = (at >= 11) & (at < 14)

    def step(k, carry):
        t = table[k]
        h, m, l = split3(t)
        low = pltpu.roll(l, 10, 0)
        both = jnp.concatenate([jnp.where(extra, low, h), jnp.where(extra, 0.0, m)], axis=1)
        pieces[pl.ds(pl.multiple_of(k * 16, 16), 16), :] = both.astype(bf16)
        return carry

    lax.fori_loop(0, rows, step, 0, unroll=4)


def lookup(pieces, rows, row, lane):
    n = row.shape[1]
    hot = jnp.where(row_iota((128, n)) == lane, 1.0, 0.0).astype(bf16)
    hot = jnp.concatenate([hot, hot], axis=0)
    row16 = jnp.broadcast_to(row, (16, n))

    def step(i, got):
        block = pieces[pl.ds(pl.multiple_of(i * 128, 128), 128), :]
        found = dot(block, hot, (1, 0))
        for u in range(8):
            got = jnp.where(row16 == i * 8 + u, found[u * 16 : u * 16 + 16], got)
        return got

    return lax.fori_loop(0, rows // 8, step, jnp.zeros((16, n), f32))


def near_item(load, ids):
    first = load(ids[0])
    is_pos = row_iota((4, WIDE)) < 3
    origin = jnp.where(is_pos, jnp.broadcast_to(first[:, 0:1], (4, WIDE)), 0.0)
    y = first - origin
    h = rnd(y)
    mid = rnd(y - h)
    fine = h + mid
    th, tm, tl = split3(square(fine))
    far_h = jnp.where(is_pos, -2.0 * h, 0.0)
    far_m = jnp.where(is_pos, -2.0 * mid, 0.0)
    one = jnp.ones((1, WIDE), f32)
    ct = pick({0: one, 1: one, 2: one, 3: th, 4: tm, 5: tl}, (8, WIDE))
    target = jnp.concatenate([far_h, far_h, far_m, far_m, ct], axis=0).astype(bf16)
    total = jnp.zeros((16, WIDE), f32)
    for k in range(4):
        raw = first if k == 0 else load(ids[k])
        ys = raw - origin
        sh = rnd(ys)
        sm = rnd(ys - sh)
        sf = sh + sm
        qh, qm, ql = split3(square(sf) + soften)
        cs = pick({0: qh, 1: qm, 2: ql, 3: one, 4: one, 5: one}, (8, WIDE))
        source = jnp.concatenate([sh, sm, sh, sm, cs], axis=0)
        r = lax.rsqrt(dot(source, target, (0, 0)))
        w = (r * r * r).astype(bf16)
        z = jnp.where(is_pos, sf * raw[3:4], raw)
        zh, zm, zl = split3(z)
        left = jnp.concatenate([zh, zm, zl, jnp.zeros((4, WIDE), f32)], axis=0)
        total = total + dot(left, w, (1, 0))
    s = total[0:4] + total[4:8] + total[8:12]
    return s - fine * s[3:4], origin, y


def far_item(cells, origin, y):
    o = [jnp.broadcast_to(origin[i : i + 1, 0:1], (1, 128)) for i in range(3)]
    mass = cells[0:1]
    px, py, pz = [cells[1 + c : 2 + c] + cells[11 + c : 12 + c] - o[c] for c in range(3)]
    trace = cells[4:5] + cells[5:6] + cells[6:7]
    qxx, qyy, qzz = [3.0 * cells[i : i + 1] - trace for i in (4, 5, 6)]
    qxy, qxz, qyz = [3.0 * cells[i : i + 1] for i in (7, 8, 9)]
    gx = qxx * px + qxy * py + qxz * pz
    gy = qxy * px + qyy * py + qyz * pz
    gz = qxz * px + qyz * py + qzz * pz
    one = jnp.ones((1, 128), f32)
    pp = px * px + py * py + pz * pz + soften
    cs = pick({0: pp, 1: -2.0 * px, 2: -2.0 * py, 3: -2.0 * pz, 4: one, 5: one, 6: one}, (16, 128))
    pg = px * gx + py * gy + pz * gz
    cq = pick(
        {0: pg, 1: -2.0 * gx, 2: -2.0 * gy, 3: -2.0 * gz, 4: qxx, 5: qyy, 6: qzz, 7: 2.0 * qxy, 8: 2.0 * qxz, 9: 2.0 * qyz},
        (16, 128),
    )
    c = jnp.concatenate([cs, cq], axis=1)
    a, b, d = y[0:1], y[1:2], y[2:3]
    ones = jnp.ones((1, WIDE), f32)
    phi = pick(
        {0: ones, 1: a, 2: b, 3: d, 4: a * a, 5: b * b, 6: d * d, 7: a * b, 8: a * d, 9: b * d}, (16, WIDE)
    )
    ch, cm, cl = split3(c)
    fh, fm, fl = split3(phi)
    sq = dot(
        jnp.concatenate([ch, ch, cm, cm, ch, cl], axis=0),
        jnp.concatenate([fh, fm, fh, fm, fl, fh], axis=0),
        (0, 0),
    )
    s, q = sq[0:128], sq[128:256]
    r = lax.rsqrt(s)
    r2 = r * r
    r3 = r * r2
    r5 = r3 * r2
    l1 = pick({0: mass * px, 1: mass * py, 2: mass * pz, 3: -mass}, (16, 128))
    l2 = pick({0: 2.5 * px, 1: 2.5 * py, 2: 2.5 * pz, 3: -2.5 * one}, (16, 128))
    l3 = pick({0: -gx, 1: -gy, 2: -gz, 4: qxx, 5: qyy, 6: qzz, 7: qxy, 8: qxz, 9: qyz}, (16, 128))
    out = jnp.zeros((32, WIDE), f32)
    for l, v in ((l1, r3), (l2, q * (r5 * r2)), (l3, r5)):
        lh = rnd(l)
        pieces = jnp.concatenate([lh, rnd(l - lh)], axis=0)
        vh = v.astype(bf16)
        vm = (v - vh.astype(f32)).astype(bf16)
        out = out + dot(
            jnp.concatenate([pieces, pieces], axis=1), jnp.concatenate([vh, vm], axis=0), (1, 0)
        )
    t = out[0:16] + out[16:32]
    axx, ayy, azz, axy, axz, ayz = [t[i : i + 1] for i in range(4, 10)]
    turned = pick(
        {0: axx * a + axy * b + axz * d, 1: axy * a + ayy * b + ayz * d, 2: axz * a + ayz * b + azz * d}, (4, WIDE)
    )
    return t[0:4] + t[3:4] * y + turned


def force_body(near, row, lane, tops, table, top, load, out, pieces, top_pieces, cells):
    spread(table, pieces, SUB * DOM)
    spread(top, top_pieces, 32)

    def gather(i, carry):
        ess = [
            lookup(pieces, SUB * DOM, row[pl.ds(2 * i + u, 1), :], lane[pl.ds(2 * i + u, 1), :])
            for u in range(2)
        ]
        t = tops[pl.ds(i, 1), :]
        far = lookup(top_pieces, 32, t >> 7, t & 127)
        blank = jnp.zeros((16, 32), f32)
        for u in range(8):
            e = ess[u // 4][:, (u % 4) * 64 : (u % 4) * 64 + 64]
            cells[i * 8 + u] = jnp.concatenate([e, far[:, u * 32 : u * 32 + 32], blank], axis=1)
        return carry

    lax.fori_loop(0, ITEMS // 8, gather, 0)

    def item(w, carry):
        acc, origin, y = near_item(load, [near[w * 4 + k] for k in range(4)])
        out[w] = acc + far_item(cells[w], origin, y)
        return carry

    lax.fori_loop(0, ITEMS, item, 0)


def force1_kernel(near, row, lane, tops, table, top, x, out, pieces, top_pieces, cells):
    force_body(near, row, lane, tops, table, top, lambda i: x[i], out, pieces, top_pieces, cells)


def force2_kernel(near, slot, row, lane, tops, table, top, x, ahead, force, out, pieces, top_pieces, cells):
    def load(i):
        p = ahead[i]
        k = slot[i]
        f = jnp.where(k >= 0, force[jnp.maximum(k, 0)], 0.0)
        moved = p + (2.0 * kick * time_step) * p[3:4] * f
        return jnp.where(row_iota((4, WIDE)) < 3, moved, x[i])

    force_body(near, row, lane, tops, table, top, load, out, pieces, top_pieces, cells)


def lists_kernel(ids, codes, row, lane):
    def one(i, carry):
        c = ids[pl.ds(i, 1), :]
        hot = jnp.where(row_iota((128, 256)) == (c & 127), 1.0, 0.0)
        r = dot((codes[...] >> 7).astype(f32), hot, (1, 0))
        l = dot((codes[...] & 127).astype(f32), hot, (1, 0))
        at = row_iota((32, 256)) == (c >> 7)
        row[pl.ds(i, 1), :] = jnp.sum(jnp.where(at, r, 0.0), axis=0, keepdims=True).astype(i32)
        lane[pl.ds(i, 1), :] = jnp.sum(jnp.where(at, l, 0.0), axis=0, keepdims=True).astype(i32)
        return carry

    lax.fori_loop(0, 10, one, 0)


V = pl.BlockSpec(memory_space=pltpu.VMEM)
S = pl.BlockSpec(memory_space=pltpu.SMEM)


def shaped(*shape, dtype=f32):
    return jax.ShapeDtypeStruct(shape, dtype)


def call(kernel, outs, places, scratch, args, **params):
    return pl.pallas_call(
        kernel,
        out_shape=outs,
        in_specs=places,
        out_specs=jax.tree.map(lambda _: V, outs),
        scratch_shapes=scratch,
        compiler_params=pltpu.CompilerParams(vmem_limit_bytes=48 * MIB, **params),
    )(*args)


def exchange_cells(rec):
    dma = pltpu.SemaphoreType.DMA
    return call(
        cells_kernel,
        (shaped(SUB, DOM, 16, 128), shaped(SUB, 4, 16, 128)),
        [V],
        [pltpu.VMEM((DOM, 16, 128), f32), pltpu.VMEM((48, 32), f32)]
        + [dma((DOM - 1,)), dma((DOM - 1,)), dma((SUB - 1,)), dma((SUB - 1,))] * 2,
        (rec,),
        collective_id=1,
        has_side_effects=True,
    )


def body(positions, velocities, masses, accel_prev, active, bucket_top, near_list, cell_list, top_list, essential, work):
    n = positions.shape[1]
    sub_index = lax.axis_index("sub")
    act = active.reshape(1, n)
    mass = masses.reshape(1, n)
    top_row = bucket_top.astype(f32).reshape(1, BUCKETS)

    wanted = essential.reshape(DOM, -1)
    codes = ((wanted >> 7) * DOM + jnp.arange(DOM, dtype=i32)[:, None]) * 128 + (wanted & 127)
    lists = jnp.concatenate([near_list, cell_list, top_list, jnp.zeros((BUCKETS, 28), i32)], axis=1)
    tail = jnp.concatenate([work, jnp.full((128 - ITEMS,), -1, i32)])[None]
    packed = jnp.concatenate([lists, codes.reshape(4, 128), tail, jnp.zeros((3, 128), i32)], axis=0)
    shared = lax.all_gather(packed, "sub", axis=0, tiled=False)
    rows = shared[:, :BUCKETS].reshape(GROUP, 128)[work]
    near = rows[:, :4].reshape(-1)
    tops = rows[:, 68:100].reshape(5, 256)
    row, lane = call(
        lists_kernel, (shaped(10, 256, dtype=i32), shaped(10, 256, dtype=i32)), [V, V], [],
        (rows[:, 4:68].reshape(10, 256), shared[:, BUCKETS : BUCKETS + 4].reshape(32, 128)),
    )
    all_work = shared[:, BUCKETS + 4, :ITEMS].reshape(-1)
    order = jnp.arange(SUB * ITEMS, dtype=i32)
    slot = jnp.max(
        jnp.where(all_work[None, :] == jnp.arange(GROUP, dtype=i32)[:, None], order[None, :], -1), axis=1
    )
    own_slot = lax.dynamic_slice(slot, (sub_index * BUCKETS,), (BUCKETS,))

    flat, boxed = shaped(3, n), shaped(BUCKETS, 4, WIDE)
    record = shaped(16, BUCKETS)
    dense = [pltpu.VMEM((4, BUCKETS, WIDE), f32)]
    half, x4, p4, rec = call(
        first_kernel, (flat, boxed, boxed, record), [V] * 6, dense,
        (positions, velocities, accel_prev, act, mass, top_row),
    )
    x = lax.all_gather(x4, "sub", axis=0, tiled=True)
    ahead = lax.all_gather(p4, "sub", axis=0, tiled=True)

    scratch = [
        pltpu.VMEM((SUB * DOM * 16, 256), bf16),
        pltpu.VMEM((32 * 16, 256), bf16),
        pltpu.VMEM((ITEMS, 16, 128), f32),
    ]

    def tables(rec):
        table, top = exchange_cells(rec)
        return table.reshape(SUB * DOM, 16, 128), top.reshape(32, 16, 128)

    acc = call(
        force1_kernel, shaped(ITEMS, 4, WIDE), [S] + [V] * 6, scratch, (near, row, lane, tops, *tables(rec), x)
    )
    force = lax.all_gather(acc, "sub", axis=0, tiled=True)
    half, places, rec = call(
        second_kernel, (flat, flat, record), [S] + [V] * 6, dense, (own_slot, x4, half, act, mass, top_row, force)
    )
    acc = call(
        force2_kernel, shaped(ITEMS, 4, WIDE), [S, S] + [V] * 8, scratch,
        (near, slot, row, lane, tops, *tables(rec), x, ahead, force),
    )
    force = lax.all_gather(acc, "sub", axis=0, tiled=True)
    speeds = call(last_kernel, flat, [S] + [V] * 3, [], (own_slot, half, act, force))
    return (speeds, places)


def solution(mesh):
    both = ("dom", "sub")
    in_specs = (
        P(None, both), P(None, both), P(both), P(None, both), P(both), P(both),
        P(both, None), P(both, None), P(both, None), P("dom", "sub", None, None), P(both),
    )
    return jax.shard_map(
        body, mesh=mesh, in_specs=in_specs, out_specs=(P(None, both), P(None, both)), check_vma=False
    )
```

time: 723 us -> 342 us (0.47)
  other arithmetic: 279 us -> 1.08 us
  Pallas kernels: 0 us -> 258 us
  local copies, waits for them, and re-layouts: 242 us -> 11.7 us
  blocking collectives: 74.1 us -> 15 us
  starting transfers between devices: 51.6 us -> 0.16 us
    pallas_call x0 -> x8, Pallas kernels: none -> 258 us  [call(): pl.pallas_call(kernel, out_shape=outs, in_specs=places, out_specs=jax.tre...]
    reduce_sum x95 -> x0, other arithmetic: 171 us -> none  [the longest x20 83.4 us: pair_accel(): distance = jnp.sum(offsets * offsets, axis=0) + soften]
    gather x127 -> x1, local copies, waits for them, and re-layouts: 158 us -> 0.58 us  [body(): rows = shared[:, :BUCKETS].reshape(GROUP, 128)[work]]
    mul x70 -> x1, other arithmetic: 65.2 us -> 0.01 us  [body(): (wanted >> 7) * DOM + jnp.arange(DOM, dtype=i32)[:, None]]
    all_to_all x10 -> x0, starting transfers between devices: 51.6 us -> none  [the longest x6 28.5 us: copy_for_each(): lax.all_to_all(jnp.broadcast_to(x[None], (count, *x.shape)), axis, 0, 0,...]
    all_to_all x3 -> x0, blocking collectives: 44.3 us -> none  [the longest x2 31.4 us: copy_for_each(): lax.all_to_all(jnp.broadcast_to(x[None], (count, *x.shape)), axis, 0, 0,...]
    all_to_all x10 -> x0, waiting for transfers between devices: 43.4 us -> none  [the longest x6 19.1 us: copy_for_each(): lax.all_to_all(jnp.broadcast_to(x[None], (count, *x.shape)), axis, 0, 0,...]
    all_gather x2 -> x4, waiting for transfers between devices: 3.96 us -> 41.5 us  [the longest x2 41.5 us: body(): force = lax.all_gather(acc, 'sub', axis=0, tiled=True)]
  transfers between devices with their start and end apart: 12 -> 4, of which waited for: 9 -> 2; matrix products, arithmetic and copies ran while one was open for 4% -> 1% of each run, Pallas kernels for 0% -> 30%
where the time goes in v1:
time: 342 us
  Pallas kernels  258 us (75%)
  waiting for transfers between devices  42.3 us (12%)
  blocking collectives  15 us (4%)
  between operations  14 us (4%)
  local copies, waits for them, and re-layouts  11.7 us (3%)
    pallas_call x8, Pallas kernels, call(): pl.pallas_call(kernel, out_shape=outs, in_specs=places, out_specs=jax.tre...  258 us
    all_gather x2, waiting for transfers between devices, body(): force = lax.all_gather(acc, 'sub', axis=0, tiled=True)  41.5 us
    all_gather x1, blocking collectives, body(): shared = lax.all_gather(packed, 'sub', axis=0, tiled=False)  15 us
    unnamed x35, local copies, waits for them, and re-layouts  10.1 us
  transfers between devices with their start and end apart: 4, of which 2 were waited for; matrix products, arithmetic and copies ran while one was open for 1% of the time, Pallas kernels for 30%

profile of v1, /device:TPU:1, one launch (start us, length us, event | category | flops | bytes accessed | tf_op | source)
XLA Modules:
  0.0 342.0 jit_solution(12174600970392032059)
XLA Ops:
  7.2 0.0 all-gather.6.cloned.1.call-start
  7.2 0.7 convert_bitcast_fusion.top_row
  7.9 0.9 copy-done.4
  8.8 1.0 copy-done.6
  9.8 1.0 copy-done.7
  10.9 1.0 copy-done.8
  11.9 0.9 copy-done.9
  12.8 2.5 shard_map.122
  15.3 0.0 all-gather.6.cloned.1.call-update
  15.3 0.0 all-gather.8.cloned.1.call-start
  15.4 0.1 pad.7.clone
  15.5 0.1 add.36
  15.6 0.1 add.37
  15.7 0.1 mul.22
  15.7 0.1 and.13
  15.8 0.1 copy.24
  15.9 0.1 copy.25
  16.0 0.1 copy.26
  16.2 0.1 add_add_fusion
  16.3 15.0 %all-gather = s32[1088,128]{1,0:T(8,128)S(1)} all-gather(s32[136,128]{1,0:T(8,128)S(1)} %add_add_fusion), channel_id=2, replica_groups=mesh['dom'=16,'sub'=8] {'sub'}, dimensions={0}, use_global_device_ids=true | all-gather | bytes 626688 | tf_op jit(solution)/shard_map/all_gather | solution.py:434
  31.4 0.6 gather_fusion
  32.0 0.1 slice.29
  32.1 0.1 slice.31
  32.1 0.1 reshape.56.near
  32.2 0.1 reshape.57.ids
  32.3 0.1 reshape.59.tops
  32.4 46.1 %shard_map.124 = (f32[8,16,16,128]{3,2,1,0:T(8,128)S(1)}, f32[8,4,16,128]{3,2,1,0:T(8,128)S(1)}) custom-call(f32[16,128]{1,0:T(8,128)S(1)} %get-tuple-element.19.rec), custom_call_target="tpu_custom_call" | custom-call | tf_op jit(solution)/shard_map/pallas_call | solution.py:398
  78.5 1.6 shard_map.123
  80.0 0.0 all-gather.6.cloned.1.call-done.x
  80.1 2.2 copy-done
  82.3 74.6 %shard_map.125 = f32[40,4,256]{2,1,0:T(4,128)} custom-call(s32[160]{0:T(256)S(1)} %reshape.56.near, s32[10,256]{1,0:T(8,128)S(1)} %get-tuple-element.17.row, s32[10,256]{1,0:T(8,128)S(1)} %get-tuple-element.18.lane, s32[5,256]{1,0:T(8,128)S(1)} %reshape.59.tops, f32[128,16,128]{2,1,0:T(8,128)S(1)} %bitcast.22, f32[32,16,128]{2,1,0:T(8,128)S(1)} %bitcast.26, ...), custom_call_target="tpu_custom_call" | custom-call | tf_op jit(solution)/shard_map/pallas_call | solution.py:398
  156.9 0.0 all-gather.8.cloned.1.call-update
  156.9 0.0 all-gather.10.cloned.1.call-start
  156.9 0.7 all-gather.10.cloned.1.call-update
  157.6 0.0 all-gather.12.cloned.1.call-start
  157.7 0.1 eq.15
  157.8 0.3 select_reduce_fusion.slot
  158.0 0.1 dynamic_slice.3.slot
  158.1 19.6 %all-gather.8.cloned.1.call-done.force = f32[320,4,256]{2,1,0:T(4,128)} async-done(((f32[40,4,256]{2,1,0:T(4,128)}), f32[320,4,256]{2,1,0:T(4,128)}) %all-gather.8.cloned.1.call-update) | async-done | bytes 1310736 | tf_op jit(solution)/shard_map/all_gather | solution.py:472
  177.7 1.3 copy-done.1
  179.0 3.8 %shard_map.126 = (f32[3,32768]{1,0:T(4,128)S(1)}, f32[3,32768]{1,0:T(4,128)}, f32[16,128]{1,0:T(8,128)S(1)}) custom-call(s32[128]{0:T(128)S(1)} %dynamic_slice.3.slot, f32[128,4,256]{2,1,0:T(4,128)} %get-tuple-element.15.x4, f32[3,32768]{1,0:T(4,128)S(1)} %get-tuple-element.16.half, s32[1,32768]{1,0:T(1,128)S(1)} %bitcast.19, f32[1,32768]{1,0:T(1,128)S(1)} %bitcast.24, ...), custom_call_target="tpu_custom_call" | custom-call | tf_op jit(solution)/shard_map/pallas_call | solution.py:398
  182.9 49.7 %shard_map.127 = (f32[8,16,16,128]{3,2,1,0:T(8,128)S(1)}, f32[8,4,16,128]{3,2,1,0:T(8,128)S(1)}) custom-call(f32[16,128]{1,0:T(8,128)S(1)} %get-tuple-element.23.rec), custom_call_target="tpu_custom_call" | custom-call | tf_op jit(solution)/shard_map/pallas_call | solution.py:398
  232.6 0.0 all-gather.10.cloned.1.call-done.ahead
  232.6 77.5 %shard_map.128 = f32[40,4,256]{2,1,0:T(4,128)} custom-call(s32[160]{0:T(256)S(1)} %reshape.56.near, s32[1024]{0:T(1024)S(1)} %select_reduce_fusion.slot, s32[10,256]{1,0:T(8,128)S(1)} %get-tuple-element.17.row, s32[10,256]{1,0:T(8,128)S(1)} %get-tuple-element.18.lane, s32[5,256]{1,0:T(8,128)S(1)} %reshape.59.tops, f32[128,16,128]{2,1,0:T(8,128)S(1)} %bitcast.21, ...), custom_call_target="tpu_custom_call" | custom-call | tf_op jit(solution)/shard_map/pallas_call | solution.py:398
  310.1 0.0 all-gather.12.cloned.1.call-update
  310.2 21.9 %all-gather.12.cloned.1.call-done.force = f32[320,4,256]{2,1,0:T(4,128)} async-done(((f32[40,4,256]{2,1,0:T(4,128)}), f32[320,4,256]{2,1,0:T(4,128)}) %all-gather.12.cloned.1.call-update) | async-done | bytes 1310736 | tf_op jit(solution)/shard_map/all_gather | solution.py:480
  332.0 1.3 copy-done.3
  333.4 2.1 shard_map.129
  (35 shorter events, 0.1 us)
Async XLA Ops:
  7.2 8.7 %copy-start.14 = (s32[128,4]{0,1:T(4,128)S(1)}, s32[128,4]{0,1:T(4,128)}, u32[]{:S(2)}) copy-start(s32[128,4]{0,1:T(4,128)} %param.17) | copy-start | bytes 6148
  7.2 72.9 %all-gather.6.cloned.1.call-start = ((), (), s32[]{:S(2)}) async-start(), calls=%async_computation | async-start | bytes 4718592 | tf_op jit(solution)/shard_map/all_gather | solution.py:456
  7.9 0.9 copy-start.4
  8.8 1.0 copy-start.6
  9.8 1.0 copy-start.7
  10.9 1.0 copy-start.8
  11.9 0.9 copy-start.9
  12.8 2.8 copy-start.13
  12.8 3.1 copy-start.11
  12.8 3.2 copy-start.12
  12.8 3.3 copy-start.15
  15.3 162.4 %all-gather.8.cloned.1.call-start = ((), (), s32[]{:S(2)}) async-start(), calls=%async_computation.1 | async-start | bytes 1474560 | tf_op jit(solution)/shard_map/all_gather | solution.py:472
  80.1 2.2 copy-start
  82.3 95.4 %copy-start.5 = (s32[32768]{0:T(1024)S(1)}, s32[32768]{0:T(1024)}, u32[]{:S(2)}) copy-start(s32[32768]{0:T(1024)} %param.15) | copy-start | bytes 393220
  82.3 95.5 %copy-start.10 = (f32[32768]{0:T(1024)S(1)}, f32[32768]{0:T(1024)}, u32[]{:S(2)}) copy-start(f32[32768]{0:T(1024)} %param.13) | copy-start | bytes 393220
  156.9 75.7 %all-gather.10.cloned.1.call-start = ((), (), s32[]{:S(2)}) async-start(), calls=%async_computation.2 | async-start | bytes 4718592 | tf_op jit(solution)/shard_map/all_gather | solution.py:457
  157.6 174.4 %all-gather.12.cloned.1.call-start = ((), (), s32[]{:S(2)}) async-start(), calls=%async_computation.3 | async-start | bytes 1474560 | tf_op jit(solution)/shard_map/all_gather | solution.py:480
  177.7 1.3 copy-start.1
  179.0 53.6 %copy-start.2 = (f32[320,4,256]{2,1,0:T(4,128)S(1)}, f32[320,4,256]{2,1,0:T(4,128)}, u32[]{:S(2)}) copy-start(f32[320,4,256]{2,1,0:T(4,128)} %all-gather.8.cloned.1.call-done.force) | copy-start | bytes 3932164
  332.0 1.3 copy-start.3
Sparse Core Ops, SparseCore 0:
  15.5 38.8 all-gather.5
  157.0 20.6 all-gather.7
  179.4 43.2 all-gather.9
  310.3 21.7 all-gather.11

commit v2 on v1

--- a/solution.py
+++ b/solution.py
@@ -17,6 +17,8 @@
 soften = 0.0025
 mass_floor = 0.5
 kick = 0.5 * time_step
+PAIRS = ((0, 0), (1, 1), (2, 2), (0, 1), (0, 2), (1, 2))
+NEAR_1, NEAR_2, NEAR_3, NEAR_4 = 8, 20, 28, 36
 
 
 def rnd(a):
@@ -70,8 +72,7 @@
     start = [total(dense[c], lead) for c in range(3)]
     s = [total(my[c]) for c in range(3)]
     d = [s[c] / mass for c in range(3)]
-    pairs = ((0, 0), (1, 1), (2, 2), (0, 1), (0, 2), (1, 2))
-    second = [total(my[a] * y[b]) - s[a] * d[b] for a, b in pairs]
+    second = [total(my[a] * y[b]) - s[a] * d[b] for a, b in PAIRS]
     rows = {0: mass, 10: top_row}
     for c in range(3):
         rows[1 + c] = start[c] + d[c]
@@ -103,7 +104,7 @@
     def one(b, carry):
         sl = pl.ds(pl.multiple_of(b * WIDE, WIDE), WIDE)
         a = act[:, sl].astype(f32)
-        f = jnp.where(slot[b] >= 0, force[jnp.maximum(slot[b], 0)][0:3], 0.0)
+        f = forced(force, slot[b])
         push = kick * a * f
         h = half[:, sl] + push + push
         x = x4[b][0:3] + time_step * h
@@ -121,7 +122,7 @@
 def last_kernel(slot, half, act, force, vel_ref):
     def one(b, carry):
         sl = pl.ds(pl.multiple_of(b * WIDE, WIDE), WIDE)
-        f = jnp.where(slot[b] >= 0, force[jnp.maximum(slot[b], 0)][0:3], 0.0)
+        f = forced(force, slot[b])
         vel_ref[:, sl] = half[:, sl] + kick * act[:, sl].astype(f32) * f
         return carry
 
@@ -135,86 +136,12 @@
     ]
 
 
-def cells_kernel(rec, out, top, part, sums, s1, r1, s2, r2, s3, r3, s4, r4):
-    g, s = lax.axis_index("dom"), lax.axis_index("sub")
-    across = [(lax.rem(g + k, DOM), s) for k in range(1, DOM)]
-    within = [(g, lax.rem(s + k, SUB)) for k in range(1, SUB)]
-    barrier = pltpu.get_barrier_semaphore()
-    for peer in across + within:
-        pl.semaphore_signal(barrier, inc=1, device_id=peer, device_id_type=MESH)
-    pl.semaphore_wait(barrier, DOM + SUB - 2)
-
-    def send(ref_from, ref_to, peers, sends, recvs):
-        copies = [
-            pltpu.make_async_remote_copy(
-                src_ref=ref_from, dst_ref=ref_to, send_sem=sends.at[k], recv_sem=recvs.at[k],
-                device_id=peer, device_id_type=MESH,
-            )
-            for k, peer in enumerate(peers)
-        ]
-        for c in copies:
-            c.start()
-        return copies
-
-    def done(copies):
-        for c in copies:
-            c.wait()
-
-    out[s, g] = rec[...]
-    done(send(rec, out.at[s, g], across, s1, r1))
-    done(send(out.at[s], out.at[s], within, s2, r2))
-
-    base = (s * DOM + g) * 32
-    ids = lax.broadcasted_iota(i32, (32, BUCKETS), 0) + base
-
-    def values(t):
-        mass = t[0:1]
-        own = t[10:11].astype(i32)
-        d = [t[1 + c : 2 + c] - at for c, at in enumerate(centre(own))]
-        md = [mass * d[c] for c in range(3)]
-        rows = {0: mass, 1: md[0], 2: md[1], 3: md[2]}
-        for k, (a, b) in enumerate(((0, 0), (1, 1), (2, 2), (0, 1), (0, 2), (1, 2))):
-            rows[4 + k] = t[4 + k : 5 + k] + md[a] * d[b]
-        pieces = jnp.concatenate(split3(pick(rows, (16, BUCKETS))), axis=0)
-        return pieces, jnp.where(ids == own, 1.0, 0.0)
-
-    sums[...] = jnp.zeros_like(sums)
-
-    def step(i, carry):
-        row, k = i // 4, (i % 4) * 4
-        got = [values(out[row, k + u]) for u in range(4)]
-        v = jnp.concatenate([a for a, _ in got], axis=1)
-        o = jnp.concatenate([b for _, b in got], axis=1)
-        sums[...] += dot(v, o, (1, 1))
-        return carry
-
-    lax.fori_loop(0, SUB * DOM // 4, step, 0)
-    t = sums[0:16] + sums[16:32] + sums[32:48]
-    mass = t[0:1]
-    w = jnp.maximum(mass, mass_floor)
-    at = centre(lax.broadcasted_iota(i32, (1, 32), 1) + base)
-    u = [t[1 + c : 2 + c] / w for c in range(3)]
-    rows = {0: mass}
-    for c in range(3):
-        rows[1 + c] = at[c] + u[c]
-    for k, (a, b) in enumerate(((0, 0), (1, 1), (2, 2), (0, 1), (0, 2), (1, 2))):
-        rows[4 + k] = t[4 + k : 5 + k] - t[1 + a : 2 + a] * u[b]
-    mine = pick(rows, (16, 32))
-    four = jnp.concatenate([mine] * 4, axis=1)
-    lane = lax.broadcasted_iota(i32, (16, 128), 1)
-    part[g] = jnp.where(lane // 32 == lax.rem(g, 4), four, 0.0)
-    done(send(part.at[g], part.at[g], across, s3, r3))
-    for k in range(4):
-        top[s, k] = part[4 * k] + part[4 * k + 1] + part[4 * k + 2] + part[4 * k + 3]
-    done(send(top.at[s], top.at[s], within, s4, r4))
-
-
 def spread(table, pieces, rows):
     at = row_iota((16, 128))
     extra = (at >= 11) & (at < 14)
 
     def step(k, carry):
-        t = table[k]
+        t = table(k)
         h, m, l = split3(t)
         low = pltpu.roll(l, 10, 0)
         both = jnp.concatenate([jnp.where(extra, low, h), jnp.where(extra, 0.0, m)], axis=1)
@@ -237,14 +164,18 @@
             got = jnp.where(row16 == i * 8 + u, found[u * 16 : u * 16 + 16], got)
         return got
 
-    return lax.fori_loop(0, rows // 8, step, jnp.zeros((16, n), f32))
+    return lax.fori_loop(0, rows // 8, step, jnp.zeros((16, n), f32), unroll=rows // 8)
+
+
+def from_first(first):
+    is_pos = row_iota((4, WIDE)) < 3
+    origin = jnp.where(is_pos, jnp.broadcast_to(first[:, 0:1], (4, WIDE)), 0.0)
+    return is_pos, origin, first - origin
 
 
 def near_item(load, ids):
     first = load(ids[0])
-    is_pos = row_iota((4, WIDE)) < 3
-    origin = jnp.where(is_pos, jnp.broadcast_to(first[:, 0:1], (4, WIDE)), 0.0)
-    y = first - origin
+    is_pos, origin, y = from_first(first)
     h = rnd(y)
     mid = rnd(y - h)
     fine = h + mid
@@ -254,7 +185,7 @@
     one = jnp.ones((1, WIDE), f32)
     ct = pick({0: one, 1: one, 2: one, 3: th, 4: tm, 5: tl}, (8, WIDE))
     target = jnp.concatenate([far_h, far_h, far_m, far_m, ct], axis=0).astype(bf16)
-    total = jnp.zeros((16, WIDE), f32)
+    total = jnp.zeros((WIDE, 16), f32)
     for k in range(4):
         raw = first if k == 0 else load(ids[k])
         ys = raw - origin
@@ -264,14 +195,15 @@
         qh, qm, ql = split3(square(sf) + soften)
         cs = pick({0: qh, 1: qm, 2: ql, 3: one, 4: one, 5: one}, (8, WIDE))
         source = jnp.concatenate([sh, sm, sh, sm, cs], axis=0)
-        r = lax.rsqrt(dot(source, target, (0, 0)))
+        r = lax.rsqrt(dot(target, source, (0, 0)))
         w = (r * r * r).astype(bf16)
         z = jnp.where(is_pos, sf * raw[3:4], raw)
         zh, zm, zl = split3(z)
         left = jnp.concatenate([zh, zm, zl, jnp.zeros((4, WIDE), f32)], axis=0)
-        total = total + dot(left, w, (1, 0))
+        total = total + dot(w, left, (1, 1))
+    total = total.T
     s = total[0:4] + total[4:8] + total[8:12]
-    return s - fine * s[3:4], origin, y
+    return s - fine * s[3:4]
 
 
 def far_item(cells, origin, y):
@@ -330,46 +262,157 @@
     return t[0:4] + t[3:4] * y + turned
 
 
-def force_body(near, row, lane, tops, table, top, load, out, pieces, top_pieces, cells):
-    spread(table, pieces, SUB * DOM)
-    spread(top, top_pieces, 32)
+def top_values(t, ids):
+    mass = t[0:1]
+    own = t[10:11].astype(i32)
+    d = [t[1 + c : 2 + c] - at for c, at in enumerate(centre(own))]
+    md = [mass * d[c] for c in range(3)]
+    rows = {0: mass, 1: md[0], 2: md[1], 3: md[2]}
+    for k, (a, b) in enumerate(PAIRS):
+        rows[4 + k] = t[4 + k : 5 + k] + md[a] * d[b]
+    pieces = jnp.concatenate(split3(pick(rows, (16, BUCKETS))), axis=0)
+    return pieces, jnp.where(ids == own, 1.0, 0.0)
+
+
+def top_record(t, base):
+    mass = t[0:1]
+    w = jnp.maximum(mass, mass_floor)
+    at = centre(lax.broadcasted_iota(i32, (1, 32), 1) + base)
+    u = [t[1 + c : 2 + c] / w for c in range(3)]
+    rows = {0: mass}
+    for c in range(3):
+        rows[1 + c] = at[c] + u[c]
+    for k, (a, b) in enumerate(PAIRS):
+        rows[4 + k] = t[4 + k : 5 + k] - t[1 + a : 2 + a] * u[b]
+    return pick(rows, (16, 32))
+
+
+def substep(near, row, lane, tops, rec, load, out, scratch):
+    (table, top, part, sums, pieces, top_pieces, cells, pairs, s1, r1, s2, r2, s3, r3, s4, r4, s5, r5, s6, r6, s7, r7) = scratch
+    g, s = lax.axis_index("dom"), lax.axis_index("sub")
+    core, chip = lax.rem(s, 2), s // 2
+    sibling = [(g, s + 1 - 2 * core)]
+    across = [(lax.rem(g + k, DOM), s) for k in range(1, DOM)]
+    within = [(g, lax.rem(s + k, SUB)) for k in range(1, SUB)]
+    along = [(g, lax.rem(s + k, SUB)) for k in (2, 6, 4)]
+    barrier = pltpu.get_barrier_semaphore()
+    for peer in across + within:
+        pl.semaphore_signal(barrier, inc=1, device_id=peer, device_id_type=MESH)
+    pl.semaphore_wait(barrier, DOM + SUB - 2)
+
+    def send(ref_from, ref_to, peers, sends, recvs):
+        copies = [
+            pltpu.make_async_remote_copy(
+                src_ref=ref_from, dst_ref=ref_to, send_sem=sends.at[k], recv_sem=recvs.at[k],
+                device_id=peer, device_id_type=MESH,
+            )
+            for k, peer in enumerate(peers)
+        ]
+        for c in copies:
+            c.start()
+        return copies
+
+    def done(copies):
+        for c in copies:
+            c.wait()
+
+    def near_part(begin, end):
+        def item(w, carry):
+            pairs[w] = near_item(load, [near[w * 4 + k] for k in range(4)])
+            return carry
+
+        lax.fori_loop(begin, end, item, 0, unroll=4)
+
+    table[core, chip, g] = rec[...]
+    flight = send(rec, table.at[core, chip, g], across, s1, r1)
+    near_part(0, NEAR_1)
+    done(flight)
+    flight = send(table.at[core, chip], table.at[core, chip], along, s2, r2)
+    near_part(NEAR_1, NEAR_2)
+    done(flight)
+    flight = send(table.at[core], table.at[core], sibling, s3, r3)
+    near_part(NEAR_2, NEAR_3)
+    done(flight)
+
+    base = (s * DOM + g) * 32
+    ids = lax.broadcasted_iota(i32, (32, BUCKETS), 0) + base
+    sums[...] = jnp.zeros_like(sums)
+
+    def step(i, carry):
+        at, k = i // 4, (i % 4) * 4
+        got = [top_values(table[at // 4, at % 4, k + u], ids) for u in range(4)]
+        v = jnp.concatenate([a for a, _ in got], axis=1)
+        o = jnp.concatenate([b for _, b in got], axis=1)
+        sums[...] += dot(v, o, (1, 1))
+        return carry
+
+    lax.fori_loop(0, SUB * DOM // 4, step, 0, unroll=4)
+    mine = top_record(sums[0:16] + sums[16:32] + sums[32:48], base)
+    four = jnp.concatenate([mine] * 4, axis=1)
+    quarter = lax.broadcasted_iota(i32, (16, 128), 1) // 32
+    part[g] = jnp.where(quarter == lax.rem(g, 4), four, 0.0)
+    flight = send(part.at[g], part.at[g], across, s4, r4)
+    near_part(NEAR_3, NEAR_4)
+    done(flight)
+    for k in range(4):
+        top[s, k] = part[4 * k] + part[4 * k + 1] + part[4 * k + 2] + part[4 * k + 3]
+    flight = send(top.at[s], top.at[s], within, s5, r5)
+
+    spread(lambda k: table[k // 64, k // 16 % 4, k % 16], pieces, SUB * DOM)
 
     def gather(i, carry):
-        ess = [
-            lookup(pieces, SUB * DOM, row[pl.ds(2 * i + u, 1), :], lane[pl.ds(2 * i + u, 1), :])
-            for u in range(2)
-        ]
+        ess = lookup(pieces, SUB * DOM, row[pl.ds(i, 1), :], lane[pl.ds(i, 1), :])
+        blank = jnp.zeros((16, 64), f32)
+        for u in range(4):
+            cells[i * 4 + u] = jnp.concatenate([ess[:, u * 64 : u * 64 + 64], blank], axis=1)
+        return carry
+
+    lax.fori_loop(0, ITEMS // 4, gather, 0)
+    near_part(NEAR_4, ITEMS)
+    done(flight)
+    spread(lambda k: top[k // 4, k % 4], top_pieces, 32)
+
+    def gather_top(i, carry):
         t = tops[pl.ds(i, 1), :]
         far = lookup(top_pieces, 32, t >> 7, t & 127)
-        blank = jnp.zeros((16, 32), f32)
+        blank = [jnp.zeros((16, n), f32) for n in (64, 32)]
         for u in range(8):
-            e = ess[u // 4][:, (u % 4) * 64 : (u % 4) * 64 + 64]
-            cells[i * 8 + u] = jnp.concatenate([e, far[:, u * 32 : u * 32 + 32], blank], axis=1)
-        return carry
-
-    lax.fori_loop(0, ITEMS // 8, gather, 0)
+            cells[i * 8 + u] += jnp.concatenate([blank[0], far[:, u * 32 : u * 32 + 32], blank[1]], axis=1)
+        return carry
+
+    lax.fori_loop(0, ITEMS // 8, gather_top, 0)
 
     def item(w, carry):
-        acc, origin, y = near_item(load, [near[w * 4 + k] for k in range(4)])
-        out[w] = acc + far_item(cells[w], origin, y)
-        return carry
-
-    lax.fori_loop(0, ITEMS, item, 0)
-
-
-def force1_kernel(near, row, lane, tops, table, top, x, out, pieces, top_pieces, cells):
-    force_body(near, row, lane, tops, table, top, lambda i: x[i], out, pieces, top_pieces, cells)
-
-
-def force2_kernel(near, slot, row, lane, tops, table, top, x, ahead, force, out, pieces, top_pieces, cells):
+        _, origin, y = from_first(load(near[w * 4]))
+        acc = pairs[w] + far_item(cells[w], origin, y)
+        for c in range(3):
+            out[core, chip, c, pl.ds(w, 1), :] = acc[c : c + 1]
+        return carry
+
+    lax.fori_loop(0, ITEMS, item, 0, unroll=4)
+    done(send(out.at[core, chip], out.at[core, chip], along, s6, r6))
+    done(send(out.at[core], out.at[core], sibling, s7, r7))
+
+
+def substep1_kernel(near, row, lane, tops, rec, x, out, *scratch):
+    substep(near, row, lane, tops, rec, lambda i: x[i], out, scratch)
+
+
+def forced(force, slot):
+    k = jnp.maximum(slot, 0)
+    block, w = k // ITEMS, lax.rem(k, ITEMS)
+    rows = [force[block // 4, lax.rem(block, 4), c, pl.ds(w, 1), :] for c in range(3)]
+    return jnp.where(slot >= 0, jnp.concatenate(rows, axis=0), 0.0)
+
+
+def substep2_kernel(near, slot, row, lane, tops, rec, x, ahead, force, out, *scratch):
     def load(i):
         p = ahead[i]
-        k = slot[i]
-        f = jnp.where(k >= 0, force[jnp.maximum(k, 0)], 0.0)
-        moved = p + (2.0 * kick * time_step) * p[3:4] * f
-        return jnp.where(row_iota((4, WIDE)) < 3, moved, x[i])
-
-    force_body(near, row, lane, tops, table, top, load, out, pieces, top_pieces, cells)
+        old = x[i]
+        moved = p[0:3] + (2.0 * kick * time_step) * p[3:4] * forced(force, slot[i])
+        return jnp.concatenate([moved, old[3:4]], axis=0)
+
+    substep(near, row, lane, tops, rec, load, out, scratch)
 
 
 def lists_kernel(ids, codes, row, lane):
@@ -405,18 +448,28 @@
     )(*args)
 
 
-def exchange_cells(rec):
-    dma = pltpu.SemaphoreType.DMA
+def exchange(kernel, places, args, collective_id):
+    peers = (DOM - 1, 3, 1, DOM - 1, SUB - 1, 3, 1)
+    scratch = [
+        pltpu.VMEM((2, SUB // 2, DOM, 16, 128), f32),
+        pltpu.VMEM((SUB, 4, 16, 128), f32),
+        pltpu.VMEM((DOM, 16, 128), f32),
+        pltpu.VMEM((48, 32), f32),
+        pltpu.VMEM((SUB * DOM * 16, 256), bf16),
+        pltpu.VMEM((32 * 16, 256), bf16),
+        pltpu.VMEM((ITEMS, 16, 128), f32),
+        pltpu.VMEM((ITEMS, 4, WIDE), f32),
+    ]
+    for n in peers:
+        scratch += [pltpu.SemaphoreType.DMA((n,))] * 2
     return call(
-        cells_kernel,
-        (shaped(SUB, DOM, 16, 128), shaped(SUB, 4, 16, 128)),
-        [V],
-        [pltpu.VMEM((DOM, 16, 128), f32), pltpu.VMEM((48, 32), f32)]
-        + [dma((DOM - 1,)), dma((DOM - 1,)), dma((SUB - 1,)), dma((SUB - 1,))] * 2,
-        (rec,),
-        collective_id=1,
-        has_side_effects=True,
-    )
+        kernel, shaped(2, SUB // 2, 3, ITEMS, WIDE), places, scratch, args,
+        collective_id=collective_id, has_side_effects=True,
+    )
+
+
+def by_core(s):
+    return (s & 1) * (SUB // 2) + (s >> 1)
 
 
 def body(positions, velocities, masses, accel_prev, active, bucket_top, near_list, cell_list, top_list, essential, work):
@@ -427,7 +480,8 @@
     top_row = bucket_top.astype(f32).reshape(1, BUCKETS)
 
     wanted = essential.reshape(DOM, -1)
-    codes = ((wanted >> 7) * DOM + jnp.arange(DOM, dtype=i32)[:, None]) * 128 + (wanted & 127)
+    device = by_core(wanted >> 7)
+    codes = (device * DOM + jnp.arange(DOM, dtype=i32)[:, None]) * 128 + (wanted & 127)
     lists = jnp.concatenate([near_list, cell_list, top_list, jnp.zeros((BUCKETS, 28), i32)], axis=1)
     tail = jnp.concatenate([work, jnp.full((128 - ITEMS,), -1, i32)])[None]
     packed = jnp.concatenate([lists, codes.reshape(4, 128), tail, jnp.zeros((3, 128), i32)], axis=0)
@@ -441,6 +495,7 @@
     )
     all_work = shared[:, BUCKETS + 4, :ITEMS].reshape(-1)
     order = jnp.arange(SUB * ITEMS, dtype=i32)
+    order = by_core(order // ITEMS) * ITEMS + order % ITEMS
     slot = jnp.max(
         jnp.where(all_work[None, :] == jnp.arange(GROUP, dtype=i32)[:, None], order[None, :], -1), axis=1
     )
@@ -456,28 +511,13 @@
     x = lax.all_gather(x4, "sub", axis=0, tiled=True)
     ahead = lax.all_gather(p4, "sub", axis=0, tiled=True)
 
-    scratch = [
-        pltpu.VMEM((SUB * DOM * 16, 256), bf16),
-        pltpu.VMEM((32 * 16, 256), bf16),
-        pltpu.VMEM((ITEMS, 16, 128), f32),
-    ]
-
-    def tables(rec):
-        table, top = exchange_cells(rec)
-        return table.reshape(SUB * DOM, 16, 128), top.reshape(32, 16, 128)
-
-    acc = call(
-        force1_kernel, shaped(ITEMS, 4, WIDE), [S] + [V] * 6, scratch, (near, row, lane, tops, *tables(rec), x)
-    )
-    force = lax.all_gather(acc, "sub", axis=0, tiled=True)
+    force = exchange(substep1_kernel, [S] + [V] * 5, (near, row, lane, tops, rec, x), 1)
     half, places, rec = call(
         second_kernel, (flat, flat, record), [S] + [V] * 6, dense, (own_slot, x4, half, act, mass, top_row, force)
     )
-    acc = call(
-        force2_kernel, shaped(ITEMS, 4, WIDE), [S, S] + [V] * 8, scratch,
-        (near, slot, row, lane, tops, *tables(rec), x, ahead, force),
-    )
-    force = lax.all_gather(acc, "sub", axis=0, tiled=True)
+    force = exchange(
+        substep2_kernel, [S, S] + [V] * 7, (near, slot, row, lane, tops, rec, x, ahead, force), 2
+    )
     speeds = call(last_kernel, flat, [S] + [V] * 3, [], (own_slot, half, act, force))
     return (speeds, places)
 

time: 342 us -> 199 us (0.58)
  Pallas kernels: 258 us -> 140 us
  waiting for transfers between devices: 42.3 us -> 16.9 us
    pallas_call x8 -> x6, Pallas kernels: 258 us -> 140 us  [call(): pl.pallas_call(kernel, out_shape=outs, in_specs=places, out_specs=jax.tre...]
    all_gather x2 -> x0, waiting for transfers between devices: 41.5 us -> none  [body(): force = lax.all_gather(acc, 'sub', axis=0, tiled=True)]
    all_gather x1, waiting for transfers between devices: 0.02 us -> 16.1 us  [body(): x = lax.all_gather(x4, 'sub', axis=0, tiled=True)]
    unnamed x35 -> x31, local copies, waits for them, and re-layouts: 10.1 us -> 9.64 us
  transfers between devices with their start and end apart: 4 -> 2, of which waited for: 2 -> 1; matrix products, arithmetic and copies ran while one was open for 1% -> 1% of each run, Pallas kernels for 30% -> 37%
where the time goes in v2:
time: 199 us; the launch traced here: 198 us
  Pallas kernels  140 us (70%)
  waiting for transfers between devices  16.9 us (8%)
  blocking collectives  15 us (8%)
  between operations  14.2 us (7%)
  local copies, waits for them, and re-layouts  11.2 us (6%)
    pallas_call x6, Pallas kernels, call(): pl.pallas_call(kernel, out_shape=outs, in_specs=places, out_specs=jax.tre...  140 us
    all_gather x1, waiting for transfers between devices, body(): x = lax.all_gather(x4, 'sub', axis=0, tiled=True)  16.1 us
    all_gather x1, blocking collectives, body(): shared = lax.all_gather(packed, 'sub', axis=0, tiled=False)  15 us
    unnamed x31, local copies, waits for them, and re-layouts  9.64 us
  transfers between devices with their start and end apart: 2, of which 1 were waited for; matrix products, arithmetic and copies ran while one was open for 1% of the time, Pallas kernels for 37%

profile of v2, /device:TPU:1, one launch (start us, length us, event | category | flops | bytes accessed | tf_op | source)
XLA Modules:
  0.0 198.3 jit_solution(12581868357197145419)
XLA Ops:
  7.2 0.0 all-gather.4.cloned.1.call-start
  7.2 0.7 convert_bitcast_fusion.top_row
  7.9 0.0 copy-start.2
  7.9 0.9 copy-done.2
  8.8 1.0 copy-done.4
  9.8 1.0 copy-done.5
  10.9 1.0 copy-done.6
  11.9 0.9 copy-done.7
  12.8 0.0 copy-start.13
  12.8 2.5 %shard_map.122 = (f32[3,32768]{1,0:T(4,128)S(1)}, f32[128,4,256]{2,1,0:T(4,128)}, f32[128,4,256]{2,1,0:T(4,128)}, f32[16,128]{1,0:T(8,128)S(1)}) custom-call(f32[3,32768]{1,0:T(4,128)S(1)} %copy-done.4, f32[3,32768]{1,0:T(4,128)S(1)} %copy-done.5, f32[3,32768]{1,0:T(4,128)S(1)} %copy-done.6, s32[1,32768]{1,0:T(1,128)S(1)} %bitcast.14, ...), custom_call_target="tpu_custom_call" | custom-call | tf_op jit(solution)/shard_map/pallas_call | solution.py:441
  15.3 0.0 all-gather.4.cloned.1.call-update
  15.4 0.0 all-gather.6.cloned.1.call-start
  15.4 0.7 all-gather.6.cloned.1.call-update
  16.1 0.0 copy-done.11
  16.1 0.1 and.42
  16.2 0.1 reshape.77
  16.3 0.1 add.74
  16.4 0.1 add.75
  16.4 0.0 copy-done.12
  16.5 0.1 copy.24
  16.6 0.0 copy-done.9
  16.6 0.1 copy.25
  16.7 0.0 copy-done.10
  16.7 0.1 copy.26
  16.8 0.1 pad.7.clone
  16.9 0.0 copy-done.13
  16.9 0.1 add_add_fusion
  17.0 15.0 %all-gather = s32[1088,128]{1,0:T(8,128)S(1)} all-gather(s32[136,128]{1,0:T(8,128)S(1)} %add_add_fusion), channel_id=2, replica_groups=mesh['dom'=16,'sub'=8] {'sub'}, dimensions={0}, use_global_device_ids=true | all-gather | bytes 626688 | tf_op jit(solution)/shard_map/all_gather | solution.py:488
  32.1 0.6 gather_fusion
  32.7 0.1 slice.29
  32.8 0.1 slice.31
  32.8 0.1 reshape.73.ids
  32.9 0.1 reshape.75.tops
  33.0 0.1 reshape.72.near
  33.1 0.1 eq.17
  33.2 1.6 shard_map.123
  34.8 0.3 select_reduce_fusion.slot
  35.0 0.1 dynamic_slice.3.slot
  35.1 16.1 %all-gather.4.cloned.1.call-done.x = f32[1024,4,256]{2,1,0:T(4,128)} async-done(((f32[128,4,256]{2,1,0:T(4,128)}), f32[1024,4,256]{2,1,0:T(4,128)}) %all-gather.4.cloned.1.call-update) | async-done | bytes 4194320 | tf_op jit(solution)/shard_map/all_gather | solution.py:511
  51.3 2.2 %copy-done = f32[1024,4,256]{2,1,0:T(4,128)S(1)} copy-done((f32[1024,4,256]{2,1,0:T(4,128)S(1)}, f32[1024,4,256]{2,1,0:T(4,128)}, u32[]{:S(2)}) %copy-start) | copy-done | bytes 4194328
  53.5 67.0 %shard_map.124.force = f32[2,4,3,40,256]{4,3,2,1,0:T(8,128)S(1)} custom-call(s32[160]{0:T(256)S(1)} %reshape.72.near, s32[10,256]{1,0:T(8,128)S(1)} %get-tuple-element.13.row, s32[10,256]{1,0:T(8,128)S(1)} %get-tuple-element.14.lane, s32[5,256]{1,0:T(8,128)S(1)} %reshape.75.tops, f32[16,128]{1,0:T(8,128)S(1)} %get-tuple-element.15.rec, ...), custom_call_target="tpu_custom_call" | custom-call | tf_op jit(solution)/shard_map/pallas_call | solution.py:441
  120.5 0.0 copy-done.3
  120.5 0.0 copy-done.8
  120.5 5.0 %shard_map.125 = (f32[3,32768]{1,0:T(4,128)S(1)}, f32[3,32768]{1,0:T(4,128)}, f32[16,128]{1,0:T(8,128)S(1)}) custom-call(s32[128]{0:T(128)S(1)} %dynamic_slice.3.slot, f32[128,4,256]{2,1,0:T(4,128)} %get-tuple-element.11.x4, f32[3,32768]{1,0:T(4,128)S(1)} %get-tuple-element.12.half, s32[1,32768]{1,0:T(1,128)S(1)} %bitcast.15, f32[1,32768]{1,0:T(1,128)S(1)} %bitcast.18, ...), custom_call_target="tpu_custom_call" | custom-call | tf_op jit(solution)/shard_map/pallas_call | solution.py:441
  125.5 0.0 copy-start.1
  125.5 2.2 %copy-done.1 = f32[1024,4,256]{2,1,0:T(4,128)S(1)} copy-done((f32[1024,4,256]{2,1,0:T(4,128)S(1)}, f32[1024,4,256]{2,1,0:T(4,128)}, u32[]{:S(2)}) %copy-start.1) | copy-done | bytes 4194328
  127.7 60.5 %shard_map.126.force = f32[2,4,3,40,256]{4,3,2,1,0:T(8,128)S(1)} custom-call(s32[160]{0:T(256)S(1)} %reshape.72.near, s32[1024]{0:T(1024)S(1)} %select_reduce_fusion.slot, s32[10,256]{1,0:T(8,128)S(1)} %get-tuple-element.13.row, s32[10,256]{1,0:T(8,128)S(1)} %get-tuple-element.14.lane, s32[5,256]{1,0:T(8,128)S(1)} %reshape.75.tops, ...), custom_call_target="tpu_custom_call" | custom-call | tf_op jit(solution)/shard_map/pallas_call | solution.py:441
  188.2 3.2 %shard_map.127 = f32[3,32768]{1,0:T(4,128)} custom-call(s32[128]{0:T(128)S(1)} %dynamic_slice.3.slot, f32[3,32768]{1,0:T(4,128)S(1)} %get-tuple-element.16.half, s32[1,32768]{1,0:T(1,128)S(1)} %bitcast.16, f32[2,4,3,40,256]{4,3,2,1,0:T(8,128)S(1)} %shard_map.126.force), custom_call_target="tpu_custom_call" | custom-call | tf_op jit(solution)/shard_map/pallas_call | solution.py:441
  (24 shorter events, 0.1 us)
Async XLA Ops:
  7.2 44.1 %all-gather.4.cloned.1.call-start = ((), (), s32[]{:S(2)}) async-start(), calls=%async_computation | async-start | bytes 4718592 | tf_op jit(solution)/shard_map/all_gather | solution.py:511
  7.9 0.9 copy-start.2
  8.8 1.0 copy-start.4
  9.8 1.0 copy-start.5
  10.9 1.0 copy-start.6
  11.9 0.9 copy-start.7
  12.8 3.3 %copy-start.11 = (s32[1,1,16,32]{3,2,1,0:T(8,128)S(1)}, s32[1,1,16,32]{3,2,1,0:T(8,128)}, u32[]{:S(2)}) copy-start(s32[1,1,16,32]{3,2,1,0:T(8,128)} %param.20) | copy-start | bytes 6148
  12.8 3.6 %copy-start.12 = (s32[128,4]{0,1:T(4,128)S(1)}, s32[128,4]{0,1:T(4,128)}, u32[]{:S(2)}) copy-start(s32[128,4]{0,1:T(4,128)} %param.17) | copy-start | bytes 6148
  12.8 3.8 %copy-start.9 = (s32[128,64]{0,1:T(8,128)S(1)}, s32[128,64]{0,1:T(8,128)}, u32[]{:S(2)}) copy-start(s32[128,64]{0,1:T(8,128)} %param.18) | copy-start | bytes 98308
  12.8 3.9 %copy-start.10 = (s32[128,32]{0,1:T(8,128)S(1)}, s32[128,32]{0,1:T(8,128)}, u32[]{:S(2)}) copy-start(s32[128,32]{0,1:T(8,128)} %param.19) | copy-start | bytes 49156
  12.8 4.0 %copy-start.13 = (s32[40]{0:T(128)S(1)}, s32[40]{0:T(128)}, u32[]{:S(2)}) copy-start(s32[40]{0:T(128)} %param.21) | copy-start | bytes 484
  15.4 110.1 %all-gather.6.cloned.1.call-start = ((), (), s32[]{:S(2)}) async-start(), calls=%async_computation.1 | async-start | bytes 4718592 | tf_op jit(solution)/shard_map/all_gather | solution.py:512
  51.3 2.2 %copy-start = (f32[1024,4,256]{2,1,0:T(4,128)S(1)}, f32[1024,4,256]{2,1,0:T(4,128)}, u32[]{:S(2)}) copy-start(f32[1024,4,256]{2,1,0:T(4,128)} %all-gather.4.cloned.1.call-done.x) | copy-start | bytes 12582916
  53.5 67.0 %copy-start.3 = (s32[32768]{0:T(1024)S(1)}, s32[32768]{0:T(1024)}, u32[]{:S(2)}) copy-start(s32[32768]{0:T(1024)} %param.15) | copy-start | bytes 393220
  53.5 67.0 %copy-start.8 = (f32[32768]{0:T(1024)S(1)}, f32[32768]{0:T(1024)}, u32[]{:S(2)}) copy-start(f32[32768]{0:T(1024)} %param.13) | copy-start | bytes 393220
  125.5 2.2 %copy-start.1 = (f32[1024,4,256]{2,1,0:T(4,128)S(1)}, f32[1024,4,256]{2,1,0:T(4,128)}, u32[]{:S(2)}) copy-start(f32[1024,4,256]{2,1,0:T(4,128)} %all-gather.4.cloned.1.call-done.x) | copy-start | bytes 12582916
Sparse Core Ops, SparseCore 0:
  15.5 35.7 all-gather.3
  53.0 36.6 all-gather.5

commit v3 on v2

v3 whole, which is shorter than its diff:
```python
import jax
import jax.numpy as jnp
from jax import lax
from jax.experimental import pallas as pl
from jax.experimental.pallas import tpu as pltpu
from jax.sharding import PartitionSpec as P

f32, bf16, i32 = jnp.float32, jnp.bfloat16, jnp.int32
MESH = pl.DeviceIdType.MESH
SUB, DOM = 8, 16
BUCKETS, WIDE, ITEMS = 128, 256, 40
GROUP = SUB * BUCKETS
TOP_SIDE = 16
MIB = 2**20

time_step = 0.01
soften = 0.0025
mass_floor = 0.5
kick = 0.5 * time_step
PAIRS = ((0, 0), (1, 1), (2, 2), (0, 1), (0, 2), (1, 2))
NEAR_AT = 96
COPIES = 128


def rnd(a):
    return a.astype(bf16).astype(f32)


def split3(a):
    h = rnd(a)
    r = a - h
    m = rnd(r)
    return h, m, rnd(r - m)


def dot(a, b, dims):
    return lax.dot_general(
        a.astype(bf16), b.astype(bf16), ((dims[:1], dims[1:]), ((), ())), preferred_element_type=f32
    )


def row_iota(shape):
    return lax.broadcasted_iota(i32, shape, 0)


def pick(rows, shape):
    at = row_iota(shape)
    out = jnp.zeros(shape, f32)
    for i, v in rows.items():
        out = jnp.where(at == i, v, out)
    return out


def square(y):
    q = y * y
    return q[0:1] + q[1:2] + q[2:3]


def moments(dense, top_row, rec_ref):
    first = [dense[c][:, 0:1] for c in range(3)]
    y = [dense[c] - first[c] for c in range(3)]
    m = dense[3]
    ones = jnp.ones((8, WIDE), f32)
    lead = jnp.where(lax.broadcasted_iota(i32, (8, WIDE), 1) == 0, 1.0, 0.0)

    def total(a, by=ones):
        return lax.dot_general(
            by, a, (((1,), (1,)), ((), ())), precision=lax.Precision.HIGHEST, preferred_element_type=f32
        )[0:1]

    my = [m * y[c] for c in range(3)]
    mass = total(m)
    start = [total(dense[c], lead) for c in range(3)]
    s = [total(my[c]) for c in range(3)]
    d = [s[c] / mass for c in range(3)]
    second = [total(my[a] * y[b]) - s[a] * d[b] for a, b in PAIRS]
    rows = {0: mass, 10: top_row}
    for c in range(3):
        rows[1 + c] = start[c] + d[c]
    for k in range(6):
        rows[4 + k] = second[k]
    rec_ref[...] = pick(rows, (16, BUCKETS))


def centre(ids):
    return [
        (part.astype(f32) + 0.5) / TOP_SIDE
        for part in (ids >> 8, (ids >> 4) & 15, ids & 15)
    ]


def spread(table, pieces, rows):
    at = row_iota((16, 128))
    extra = (at >= 11) & (at < 14)

    def step(k, carry):
        t = table(k)
        h, m, l = split3(t)
        low = pltpu.roll(l, 10, 0)
        both = jnp.concatenate([jnp.where(extra, low, h), jnp.where(extra, 0.0, m)], axis=1)
        pieces[pl.ds(pl.multiple_of(k * 16, 16), 16), :] = both.astype(bf16)
        return carry

    lax.fori_loop(0, rows, step, 0, unroll=4)


def lookup(pieces, rows, row, lane):
    n = row.shape[1]
    hot = jnp.where(row_iota((128, n)) == lane, 1.0, 0.0).astype(bf16)
    hot = jnp.concatenate([hot, hot], axis=0)
    row16 = jnp.broadcast_to(row, (16, n))

    def step(i, got):
        block = pieces[pl.ds(pl.multiple_of(i * 128, 128), 128), :]
        found = dot(block, hot, (1, 0))
        for u in range(8):
            got = jnp.where(row16 == i * 8 + u, found[u * 16 : u * 16 + 16], got)
        return got

    return lax.fori_loop(0, rows // 8, step, jnp.zeros((16, n), f32), unroll=rows // 8)


def from_first(first):
    is_pos = row_iota((4, WIDE)) < 3
    origin = jnp.where(is_pos, jnp.broadcast_to(first[:, 0:1], (4, WIDE)), 0.0)
    return is_pos, origin, first - origin


def near_item(load, ids):
    first = load(ids[0])
    is_pos, origin, y = from_first(first)
    h = rnd(y)
    mid = rnd(y - h)
    fine = h + mid
    th, tm, tl = split3(square(fine))
    far_h = jnp.where(is_pos, -2.0 * h, 0.0)
    far_m = jnp.where(is_pos, -2.0 * mid, 0.0)
    one = jnp.ones((1, WIDE), f32)
    ct = pick({0: one, 1: one, 2: one, 3: th, 4: tm, 5: tl}, (8, WIDE))
    target = jnp.concatenate([far_h, far_h, far_m, far_m, ct], axis=0).astype(bf16)
    total = jnp.zeros((WIDE, 16), f32)
    for k in range(4):
        raw = first if k == 0 else load(ids[k])
        ys = raw - origin
        sh = rnd(ys)
        sm = rnd(ys - sh)
        sf = sh + sm
        qh, qm, ql = split3(square(sf) + soften)
        cs = pick({0: qh, 1: qm, 2: ql, 3: one, 4: one, 5: one}, (8, WIDE))
        source = jnp.concatenate([sh, sm, sh, sm, cs], axis=0)
        r = lax.rsqrt(dot(target, source, (0, 0)))
        w = (r * r * r).astype(bf16)
        z = jnp.where(is_pos, sf * raw[3:4], raw)
        zh, zm, zl = split3(z)
        left = jnp.concatenate([zh, zm, zl, jnp.zeros((4, WIDE), f32)], axis=0)
        total = total + dot(w, left, (1, 1))
    total = total.T
    s = total[0:4] + total[4:8] + total[8:12]
    return s - fine * s[3:4]


def far_item(cells, origin, y):
    o = [jnp.broadcast_to(origin[i : i + 1, 0:1], (1, 128)) for i in range(3)]
    mass = cells[0:1]
    px, py, pz = [cells[1 + c : 2 + c] + cells[11 + c : 12 + c] - o[c] for c in range(3)]
    trace = cells[4:5] + cells[5:6] + cells[6:7]
    qxx, qyy, qzz = [3.0 * cells[i : i + 1] - trace for i in (4, 5, 6)]
    qxy, qxz, qyz = [3.0 * cells[i : i + 1] for i in (7, 8, 9)]
    gx = qxx * px + qxy * py + qxz * pz
    gy = qxy * px + qyy * py + qyz * pz
    gz = qxz * px + qyz * py + qzz * pz
    one = jnp.ones((1, 128), f32)
    pp = px * px + py * py + pz * pz + soften
    cs = pick({0: pp, 1: -2.0 * px, 2: -2.0 * py, 3: -2.0 * pz, 4: one, 5: one, 6: one}, (16, 128))
    pg = px * gx + py * gy + pz * gz
    cq = pick(
        {0: pg, 1: -2.0 * gx, 2: -2.0 * gy, 3: -2.0 * gz, 4: qxx, 5: qyy, 6: qzz, 7: 2.0 * qxy, 8: 2.0 * qxz, 9: 2.0 * qyz},
        (16, 128),
    )
    c = jnp.concatenate([cs, cq], axis=1)
    a, b, d = y[0:1], y[1:2], y[2:3]
    ones = jnp.ones((1, WIDE), f32)
    phi = pick(
        {0: ones, 1: a, 2: b, 3: d, 4: a * a, 5: b * b, 6: d * d, 7: a * b, 8: a * d, 9: b * d}, (16, WIDE)
    )
    ch, cm, cl = split3(c)
    fh, fm, fl = split3(phi)
    sq = dot(
        jnp.concatenate([ch, ch, cm, cm, ch, cl], axis=0),
        jnp.concatenate([fh, fm, fh, fm, fl, fh], axis=0),
        (0, 0),
    )
    s, q = sq[0:128], sq[128:256]
    r = lax.rsqrt(s)
    r2 = r * r
    r3 = r * r2
    r5 = r3 * r2
    l1 = pick({0: mass * px, 1: mass * py, 2: mass * pz, 3: -mass}, (16, 128))
    l2 = pick({0: 2.5 * px, 1: 2.5 * py, 2: 2.5 * pz, 3: -2.5 * one}, (16, 128))
    l3 = pick({0: -gx, 1: -gy, 2: -gz, 4: qxx, 5: qyy, 6: qzz, 7: qxy, 8: qxz, 9: qyz}, (16, 128))
    out = jnp.zeros((32, WIDE), f32)
    for l, v in ((l1, r3), (l2, q * (r5 * r2)), (l3, r5)):
        lh = rnd(l)
        pieces = jnp.concatenate([lh, rnd(l - lh)], axis=0)
        vh = v.astype(bf16)
        vm = (v - vh.astype(f32)).astype(bf16)
        out = out + dot(
            jnp.concatenate([pieces, pieces], axis=1), jnp.concatenate([vh, vm], axis=0), (1, 0)
        )
    t = out[0:16] + out[16:32]
    axx, ayy, azz, axy, axz, ayz = [t[i : i + 1] for i in range(4, 10)]
    turned = pick(
        {0: axx * a + axy * b + axz * d, 1: axy * a + ayy * b + ayz * d, 2: axz * a + ayz * b + azz * d}, (4, WIDE)
    )
    return t[0:4] + t[3:4] * y + turned


def top_values(t, ids):
    mass = t[0:1]
    own = t[10:11].astype(i32)
    d = [t[1 + c : 2 + c] - at for c, at in enumerate(centre(own))]
    md = [mass * d[c] for c in range(3)]
    rows = {0: mass, 1: md[0], 2: md[1], 3: md[2]}
    for k, (a, b) in enumerate(PAIRS):
        rows[4 + k] = t[4 + k : 5 + k] + md[a] * d[b]
    pieces = jnp.concatenate(split3(pick(rows, (16, BUCKETS))), axis=0)
    return pieces, jnp.where(ids == own, 1.0, 0.0)


def top_record(t, base):
    mass = t[0:1]
    w = jnp.maximum(mass, mass_floor)
    at = centre(lax.broadcasted_iota(i32, (1, 32), 1) + base)
    u = [t[1 + c : 2 + c] / w for c in range(3)]
    rows = {0: mass}
    for c in range(3):
        rows[1 + c] = at[c] + u[c]
    for k, (a, b) in enumerate(PAIRS):
        rows[4 + k] = t[4 + k : 5 + k] - t[1 + a : 2 + a] * u[b]
    return pick(rows, (16, 32))


def forced(force, slot):
    k = jnp.maximum(slot, 0)
    block, w = k // ITEMS, lax.rem(k, ITEMS)
    rows = [force[block // 4, lax.rem(block, 4), c, pl.ds(w, 1), :] for c in range(3)]
    return jnp.where(slot >= 0, jnp.concatenate(rows, axis=0), 0.0)


def kernel(
    work, pos_in, vel_in, acc_in, act_in, mass_in, top_row, packed,
    vel_out, pos_out,
    pos, vel, acc, act, mass, half, dense, x, ahead,
    table_1, top_1, part_1, force_1, table_2, top_2, part_2, force_2,
    sums, pieces, top_pieces, cells, pairs,
    lists, wanted, codes, row, lane, tops, slots, near_s, work_s, slot_s,
    load_sem, send_sem, recv_sem, local_sem,
):
    g, s = lax.axis_index("dom"), lax.axis_index("sub")
    core, chip = lax.rem(s, 2), s // 2
    sibling = (g, s + 1 - 2 * core)
    up, down, over = [(g, lax.rem(s + k, SUB)) for k in (2, 6, 4)]
    along = [up, down, over]
    across = [(lax.rem(g + k, DOM), s) for k in range(1, DOM)]
    within = [(g, lax.rem(s + k, SUB)) for k in range(1, SUB)]
    used = [0]

    inputs = [
        pltpu.make_async_copy(a, b, load_sem.at[k])
        for k, (a, b) in enumerate(((pos_in, pos), (vel_in, vel), (acc_in, acc), (act_in, act), (mass_in, mass)))
    ]
    for c in inputs:
        c.start()

    barrier = pltpu.get_barrier_semaphore()
    for peer in across + within:
        pl.semaphore_signal(barrier, inc=1, device_id=peer, device_id_type=MESH)
    pl.semaphore_wait(barrier, DOM + SUB - 2)

    def send(ref, peers, source=None):
        copies = []
        for peer in peers:
            k = used[0]
            used[0] += 1
            copies.append(
                pltpu.make_async_remote_copy(
                    src_ref=ref if source is None else source, dst_ref=ref, send_sem=send_sem.at[k],
                    recv_sem=recv_sem.at[k], device_id=peer, device_id_type=MESH,
                )
            )
            copies[-1].start()
        return copies

    def done(copies):
        for c in copies:
            c.wait()

    below, above, facing = [lax.rem(chip + k, 4) for k in (3, 1, 2)]
    low, high = pl.ds(0, BUCKETS // 2), pl.ds(BUCKETS // 2, BUCKETS // 2)

    def ring_1(buf):
        return send(buf.at[core, chip], [up, down, sibling])

    def ring_2(buf, first):
        first[0].wait_recv()
        found = send(buf.at[core, below, low], [up])
        more = send(buf.at[core, below], [sibling])
        first[1].wait_recv()
        found += send(buf.at[core, above, high], [down])
        more += send(buf.at[core, above], [sibling])
        return found, more

    def ring_3(buf, first, second):
        found, more = second
        for c in found:
            c.wait_recv()
        final = send(buf.at[core, facing], [sibling])
        for c in first + found:
            c.wait_send()
        first[2].wait_recv()
        done(more)
        return final

    list_copies = send(lists.at[core, chip], along, packed)
    for c in inputs:
        c.wait()

    def first(b, carry):
        sl = pl.ds(pl.multiple_of(b * WIDE, WIDE), WIDE)
        a = act[:, sl].astype(f32)
        h = vel[:, sl] + kick * a * acc[:, sl]
        p = pos[:, sl] + time_step * h
        half[:, sl] = h
        m = mass[:, sl]
        x[core, chip, b] = jnp.concatenate([p, m], axis=0)
        ahead[core, chip, b] = jnp.concatenate([p + time_step * h, a], axis=0)
        for c in range(3):
            dense[c, pl.ds(b, 1), :] = p[c : c + 1]
        dense[3, pl.ds(b, 1), :] = m
        return carry

    lax.fori_loop(0, BUCKETS, first, 0, unroll=4)
    x_1 = ring_1(x)
    lists[core, chip] = packed[...]

    def near_part(load, begin, end):
        def item(w, carry):
            pairs[w] = near_item(load, [near_s[w, NEAR_AT + k] for k in range(4)])
            return carry

        lax.fori_loop(begin, end, item, 0, unroll=4)

    def top_sums(table, part):
        base = (s * DOM + g) * 32
        ids = lax.broadcasted_iota(i32, (32, BUCKETS), 0) + base
        sums[...] = jnp.zeros_like(sums)

        def step(i, carry):
            at, k = i // 4, (i % 4) * 4
            got = [top_values(table[at // 4, at % 4, k + u], ids) for u in range(4)]
            v = jnp.concatenate([a for a, _ in got], axis=1)
            o = jnp.concatenate([b for _, b in got], axis=1)
            sums[...] += dot(v, o, (1, 1))
            return carry

        lax.fori_loop(0, SUB * DOM // 4, step, 0, unroll=4)
        mine = top_record(sums[0:16] + sums[16:32] + sums[32:48], base)
        four = jnp.concatenate([mine] * 4, axis=1)
        quarter = lax.broadcasted_iota(i32, (16, 128), 1) // 32
        part[g] = jnp.where(quarter == lax.rem(g, 4), four, 0.0)

    def four_parts(top, part):
        for k in range(4):
            top[s, k] = part[4 * k] + part[4 * k + 1] + part[4 * k + 2] + part[4 * k + 3]

    def essential_cells(table):
        spread(lambda k: table[k // 64, k // 16 % 4, k % 16], pieces, SUB * DOM)

        def gather(i, carry):
            ess = lookup(pieces, SUB * DOM, row[pl.ds(i, 1), :], lane[pl.ds(i, 1), :])
            blank = jnp.zeros((16, 64), f32)
            for u in range(4):
                cells[i * 4 + u] = jnp.concatenate([ess[:, u * 64 : u * 64 + 64], blank], axis=1)
            return carry

        lax.fori_loop(0, ITEMS // 4, gather, 0)

    def top_cells(top):
        spread(lambda k: top[k // 4, k % 4], top_pieces, 32)

        def gather(i, carry):
            t = tops[pl.ds(i, 1), :]
            far = lookup(top_pieces, 32, t >> 7, t & 127)
            blank = [jnp.zeros((16, n), f32) for n in (64, 32)]
            for u in range(8):
                cells[i * 8 + u] += jnp.concatenate([blank[0], far[:, u * 32 : u * 32 + 32], blank[1]], axis=1)
            return carry

        lax.fori_loop(0, ITEMS // 8, gather, 0)

    def far_and_return(load, force):
        def item(w, carry):
            _, origin, y = from_first(load(near_s[w, NEAR_AT]))
            a = pairs[w] + far_item(cells[w], origin, y)
            for c in range(3):
                force[core, chip, c, pl.ds(w, 1), :] = a[c : c + 1]
            return carry

        cuts, flights = (0, 24, ITEMS), []
        for begin, end in zip(cuts, cuts[1:]):
            lax.fori_loop(begin, end, item, 0, unroll=4)
            flights.append(send(force.at[core, chip, :, pl.ds(begin, end - begin), :], along))
        last = []
        for (begin, end), flight in zip(zip(cuts, cuts[1:]), flights):
            done(flight)
            last += send(force.at[core, :, :, pl.ds(begin, end - begin), :], [sibling])
        done(last)

    moments(dense, top_row[...], table_1.at[core, chip, g])
    flight = send(table_1.at[core, chip, g], across)
    done(list_copies)
    list_copies = send(lists.at[core], [sibling])
    done(flight)
    flight = send(table_1.at[core, chip], along)
    done(list_copies)

    def take(w, carry):
        n = work[w]
        wanted[pl.ds(w, 1), :] = lists[(n >> 7) & 1, n >> 8, pl.ds(n & 127, 1), :]
        return carry

    lax.fori_loop(0, ITEMS, take, 0, unroll=4)
    to_scalars = [pltpu.make_async_copy(wanted, near_s, local_sem.at[0])]
    for k in range(SUB):
        to_scalars.append(
            pltpu.make_async_copy(lists.at[k // 4, k % 4, pl.ds(128, 8)], work_s.at[k], local_sem.at[1 + k])
        )
    for c in to_scalars:
        c.start()
    for k in range(SUB):
        codes[4 * k : 4 * k + 4, :] = lists[k % 2, k // 2, 128:132, :]

    def place(i, carry):
        ids = jnp.concatenate([wanted[pl.ds(4 * i + u, 1), :][:, 0:64] for u in range(4)], axis=1)
        hot = jnp.where(row_iota((128, 256)) == (ids & 127), 1.0, 0.0)
        at = row_iota((32, 256)) == (ids >> 7)
        for got, where in ((codes[...] >> 7, row), (codes[...] & 127, lane)):
            found = dot(got.astype(f32), hot, (1, 0))
            where[pl.ds(i, 1), :] = jnp.sum(jnp.where(at, found, 0.0), axis=0, keepdims=True).astype(i32)
        return carry

    lax.fori_loop(0, ITEMS // 4, place, 0)
    for i in range(ITEMS // 8):
        tops[i : i + 1, :] = jnp.concatenate([wanted[8 * i + u : 8 * i + u + 1, 64:96] for u in range(8)], axis=1)
    x_2 = ring_2(x, x_1)
    for c in to_scalars:
        c.wait()
    number = row_iota((SUB, 128)) * 128 + lax.broadcasted_iota(i32, (SUB, 128), 1)

    def find(w, found):
        for k in range(SUB):
            found = jnp.where(number == work_s[k, 4, w], k * ITEMS + w, found)
        return found

    slots[...] = lax.fori_loop(0, ITEMS, find, jnp.full((SUB, 128), -1, i32))
    slot_copy = pltpu.make_async_copy(slots, slot_s, local_sem.at[9])
    slot_copy.start()

    done(flight)
    flight = send(table_1.at[core], [sibling])
    x_3 = ring_3(x, x_1, x_2)
    done(flight)
    top_sums(table_1, part_1)
    flight = send(part_1.at[g], across)
    essential_cells(table_1)
    done(x_3)
    ahead_1 = ring_1(ahead)
    done(flight)
    four_parts(top_1, part_1)
    flight = send(top_1.at[s], within)

    def load_1(n):
        return x[(n >> 7) & 1, n >> 8, n & 127]

    near_part(load_1, 0, 24)
    ahead_2 = ring_2(ahead, ahead_1)
    near_part(load_1, 24, ITEMS)
    done(flight)
    top_cells(top_1)
    ahead_3 = ring_3(ahead, ahead_1, ahead_2)
    far_and_return(load_1, force_1)
    slot_copy.wait()

    def second(b, carry):
        sl = pl.ds(pl.multiple_of(b * WIDE, WIDE), WIDE)
        push = kick * act[:, sl].astype(f32) * forced(force_1, slot_s[s, b])
        h = half[:, sl] + push + push
        p = x[core, chip, b][0:3] + time_step * h
        half[:, sl] = h
        pos_out[:, sl] = p
        for c in range(3):
            dense[c, pl.ds(b, 1), :] = p[c : c + 1]
        return carry

    lax.fori_loop(0, BUCKETS, second, 0, unroll=4)
    moments(dense, top_row[...], table_2.at[core, chip, g])
    flight = send(table_2.at[core, chip, g], across)
    done(ahead_3)

    def load_2(n):
        at = ((n >> 7) & 1, n >> 8, n & 127)
        p = ahead[at]
        moved = p[0:3] + (2.0 * kick * time_step) * p[3:4] * forced(force_1, slot_s[n >> 7, n & 127])
        return jnp.concatenate([moved, x[at][3:4]], axis=0)

    near_part(load_2, 0, 8)
    done(flight)
    flight = send(table_2.at[core, chip], along)
    near_part(load_2, 8, 24)
    done(flight)
    flight = send(table_2.at[core], [sibling])
    near_part(load_2, 24, 32)
    done(flight)
    top_sums(table_2, part_2)
    flight = send(part_2.at[g], across)
    near_part(load_2, 32, ITEMS)
    done(flight)
    four_parts(top_2, part_2)
    flight = send(top_2.at[s], within)
    essential_cells(table_2)
    done(flight)
    top_cells(top_2)
    far_and_return(load_2, force_2)

    def last(b, carry):
        sl = pl.ds(pl.multiple_of(b * WIDE, WIDE), WIDE)
        vel_out[:, sl] = half[:, sl] + kick * act[:, sl].astype(f32) * forced(force_2, slot_s[s, b])
        return carry

    lax.fori_loop(0, BUCKETS, last, 0, unroll=4)


def by_core(s):
    return (s & 1) * (SUB // 2) + (s >> 1)


def body(positions, velocities, masses, accel_prev, active, bucket_top, near_list, cell_list, top_list, essential, work):
    n = positions.shape[1]
    wanted = essential.reshape(DOM, -1)
    codes = (by_core(wanted >> 7) * DOM + jnp.arange(DOM, dtype=i32)[:, None]) * 128 + (wanted & 127)
    lists = jnp.concatenate([cell_list, top_list, near_list, jnp.zeros((BUCKETS, 28), i32)], axis=1)
    tail = jnp.concatenate([work, jnp.full((128 - ITEMS,), -1, i32)])[None]
    packed = jnp.concatenate([lists, codes.reshape(4, 128), tail, jnp.zeros((3, 128), i32)], axis=0)

    vm, dma = pltpu.VMEM, pltpu.SemaphoreType.DMA
    flat = vm((3, n), f32)
    group = vm((2, SUB // 2, BUCKETS, 4, WIDE), f32)
    twice = [
        vm((2, SUB // 2, DOM, 16, 128), f32), vm((SUB, 4, 16, 128), f32), vm((DOM, 16, 128), f32),
        vm((2, SUB // 2, 3, ITEMS, WIDE), f32),
    ]
    scratch = [flat, flat, flat, vm((1, n), i32), vm((1, n), f32), flat, vm((4, BUCKETS, WIDE), f32), group, group]
    scratch += twice + twice
    scratch += [
        vm((48, 32), f32), vm((SUB * DOM * 16, 256), bf16), vm((32 * 16, 256), bf16),
        vm((ITEMS, 16, 128), f32), vm((ITEMS, 4, WIDE), f32),
        vm((2, SUB // 2, BUCKETS + 8, 128), i32), vm((ITEMS, 128), i32), vm((32, 128), i32),
        vm((16, 256), i32), vm((16, 256), i32), vm((8, 256), i32), vm((SUB, 128), i32),
        pltpu.SMEM((ITEMS, 128), i32), pltpu.SMEM((SUB, 8, 128), i32), pltpu.SMEM((SUB, 128), i32),
        dma((5,)), dma((COPIES,)), dma((COPIES,)), dma((10,)),
    ]
    place = lambda where: pl.BlockSpec(memory_space=where)
    shape = jax.ShapeDtypeStruct((3, n), f32)
    return pl.pallas_call(
        kernel,
        out_shape=(shape, shape),
        in_specs=[place(pltpu.SMEM)] + [place(pltpu.HBM)] * 5 + [place(pltpu.VMEM)] * 2,
        out_specs=(place(pltpu.VMEM), place(pltpu.VMEM)),
        scratch_shapes=scratch,
        compiler_params=pltpu.CompilerParams(collective_id=1, has_side_effects=True, vmem_limit_bytes=50 * MIB),
    )(
        work, positions, velocities, accel_prev, active.reshape(1, n), masses.reshape(1, n),
        bucket_top.astype(f32).reshape(1, BUCKETS), packed,
    )


def solution(mesh):
    both = ("dom", "sub")
    in_specs = (
        P(None, both), P(None, both), P(both), P(None, both), P(both), P(both),
        P(both, None), P(both, None), P(both, None), P("dom", "sub", None, None), P(both),
    )
    return jax.shard_map(
        body, mesh=mesh, in_specs=in_specs, out_specs=(P(None, both), P(None, both)), check_vma=False
    )
```

time: 199 us -> 162 us (0.81)
  waiting for transfers between devices: 16.9 us -> 0 us
  blocking collectives: 15 us -> 0 us
  between operations: 14.2 us -> 0.7 us
  Pallas kernels: 140 us -> 151 us
  local copies, waits for them, and re-layouts: 11.2 us -> 8.83 us
    all_gather x2 -> x0, waiting for transfers between devices: 16.1 us -> none  [the longest x1 16.1 us: body(): x = lax.all_gather(x4, 'sub', axis=0, tiled=True)]
    all_gather x1 -> x0, blocking collectives: 15 us -> none  [body(): shared = lax.all_gather(packed, 'sub', axis=0, tiled=False)]
    pallas_call x6 -> x1, Pallas kernels: 140 us -> 151 us  [body(): pl.pallas_call(kernel, out_shape=(shape, shape), in_specs=[place(pltpu.SM...]
    unnamed x31 -> x17, local copies, waits for them, and re-layouts: 9.64 us -> 7.77 us
  transfers between devices with their start and end apart: 2 -> 0, of which waited for: 1 -> 0; matrix products, arithmetic and copies ran while one was open for 1% -> 0% of each run, Pallas kernels for 37% -> 0%
where the time goes in v3:
time: 162 us
  Pallas kernels  151 us (93%)
  local copies, waits for them, and re-layouts  8.83 us (5%)
    pallas_call x1, Pallas kernels, body(): pl.pallas_call(kernel, out_shape=(shape, shape), in_specs=[place(pltpu.SM...  151 us
    unnamed x17, local copies, waits for them, and re-layouts  7.77 us

profile of v3, /device:TPU:1, one launch (start us, length us, event | category | flops | bytes accessed | tf_op | source)
XLA Modules:
  0.0 161.6 jit_solution(14332385821068420163)
XLA Ops:
  0.6 0.0 copy-start
  0.6 0.7 convert_bitcast_fusion.top_row
  1.4 0.7 pad_bitcast_fusion
  2.0 0.1 pad.7.clone
  2.1 0.1 add.36
  2.2 0.1 add.37
  2.3 0.7 add_multiply_fusion
  3.0 0.1 reshape.33
  3.0 0.1 and.18
  3.1 0.8 copy.15
  3.9 0.8 copy.13
  4.8 0.8 copy.14
  5.6 0.0 copy-start.3
  5.6 0.0 copy-start.5
  5.6 0.1 add_add_fusion.packed
  5.8 0.0 copy-done
  5.8 0.7 copy-done.3
  6.5 0.0 copy-done.5
  6.5 0.0 copy-start.1
  6.5 1.0 copy-done.1
  7.6 0.0 copy-start.2
  7.6 1.0 copy-done.2
  8.6 0.0 copy-start.4
  8.6 0.9 copy-done.4
  9.5 150.5 %shard_map.122 = (f32[3,32768]{1,0:T(4,128)S(1)}, f32[3,32768]{1,0:T(4,128)S(1)}) custom-call(s32[40]{0:T(128)S(1)} %copy-done.5, f32[3,32768]{1,0:T(4,128)S(1)} %copy-done, f32[3,32768]{1,0:T(4,128)S(1)} %copy-done.1, f32[3,32768]{1,0:T(4,128)S(1)} %copy-done.2, s32[1,32768]{1,0:T(1,128)S(1)} %bitcast.10, f32[1,32768]{1,0:T(1,128)S(1)} %bitcast.11, ...), custom_call_target="tpu_custom_call" | custom-call | tf_op jit(solution)/shard_map/pallas_call | solution.py:574
  160.0 0.8 copy.18
  160.8 0.8 copy.19
  (4 shorter events, 0.0 us)
Async XLA Ops:
  0.6 5.1 %copy-start = (f32[3,32768]{1,0:T(4,128)S(1)}, f32[3,32768]{1,0:T(4,128)}, u32[]{:S(2)}) copy-start(f32[3,32768]{1,0:T(4,128)} %pos_in.1) | copy-start | bytes 1179652
  5.6 0.9 copy-start.3
  5.6 0.9 copy-start.5
  6.5 1.0 copy-start.1
  7.6 1.0 copy-start.2
  8.6 0.9 copy-start.4

commit v4 on v3

--- a/solution.py
+++ b/solution.py
@@ -1,3 +1,5 @@
+import functools
+
 import jax
 import jax.numpy as jnp
 from jax import lax
@@ -19,7 +21,7 @@
 kick = 0.5 * time_step
 PAIRS = ((0, 0), (1, 1), (2, 2), (0, 1), (0, 2), (1, 2))
 NEAR_AT = 96
-COPIES = 128
+COPIES = 160
 
 
 def rnd(a):
@@ -240,6 +242,10 @@
     return pick(rows, (16, 32))
 
 
+def by_core(s):
+    return (s & 1) * (SUB // 2) + (s >> 1)
+
+
 def forced(force, slot):
     k = jnp.maximum(slot, 0)
     block, w = k // ITEMS, lax.rem(k, ITEMS)
@@ -248,7 +254,7 @@
 
 
 def kernel(
-    work, pos_in, vel_in, acc_in, act_in, mass_in, top_row, packed,
+    work, pos_in, vel_in, acc_in, act_in, mass_in, top_row, cell_list, top_list, near_list, requests, work_row,
     vel_out, pos_out,
     pos, vel, acc, act, mass, half, dense, x, ahead,
     table_1, top_1, part_1, force_1, table_2, top_2, part_2, force_2,
@@ -275,8 +281,6 @@
     barrier = pltpu.get_barrier_semaphore()
     for peer in across + within:
         pl.semaphore_signal(barrier, inc=1, device_id=peer, device_id_type=MESH)
-    pl.semaphore_wait(barrier, DOM + SUB - 2)
-
     def send(ref, peers, source=None):
         copies = []
         for peer in peers:
@@ -321,7 +325,6 @@
         done(more)
         return final
 
-    list_copies = send(lists.at[core, chip], along, packed)
     for c in inputs:
         c.wait()
 
@@ -340,8 +343,16 @@
         return carry
 
     lax.fori_loop(0, BUCKETS, first, 0, unroll=4)
+    pl.semaphore_wait(barrier, DOM + SUB - 2)
     x_1 = ring_1(x)
-    lists[core, chip] = packed[...]
+    turned = [cell_list[...], top_list[...], near_list[...], jnp.zeros((28, BUCKETS), i32)]
+    lists[core, chip, 0:BUCKETS, :] = jnp.concatenate(turned, axis=0).T
+    asked = requests[...]
+    asked = (by_core(asked >> 7) * DOM + row_iota((DOM, 32))) * 128 + (asked & 127)
+    rest = [jnp.concatenate([asked[4 * r + k : 4 * r + k + 1] for k in range(4)], axis=1) for r in range(4)]
+    rest.append(jnp.concatenate([work_row[...], jnp.full((1, 128 - ITEMS), -1, i32)], axis=1))
+    lists[core, chip, BUCKETS : BUCKETS + 8, :] = jnp.concatenate(rest + [jnp.zeros((3, 128), i32)], axis=0)
+    list_copies = send(lists.at[core, chip], along)
 
     def near_part(load, begin, end):
         def item(w, carry):
@@ -398,30 +409,73 @@
 
         lax.fori_loop(0, ITEMS // 8, gather, 0)
 
-    def far_and_return(load, force):
-        def item(w, carry):
-            _, origin, y = from_first(load(near_s[w, NEAR_AT]))
-            a = pairs[w] + far_item(cells[w], origin, y)
-            for c in range(3):
-                force[core, chip, c, pl.ds(w, 1), :] = a[c : c + 1]
+    def finish(load, force, known):
+        first_sem = used[0]
+        used[0] += 16
+
+        def copy(ref, k, peer):
+            return pltpu.make_async_remote_copy(
+                src_ref=ref, dst_ref=ref, send_sem=send_sem.at[k], recv_sem=recv_sem.at[k],
+                device_id=peer, device_id_type=MESH,
+            )
+
+        def rows(p):
+            return pl.ds(pl.multiple_of(p * 8, 8), 8)
+
+        def by_links(p):
+            ref = force.at[core, chip, :, rows(p), :]
+            return [copy(ref, first_sem + p * 3 + k, peer) for k, peer in enumerate(along)]
+
+        def to_sibling(p):
+            return copy(force.at[core, :, :, rows(p), :], first_sem + 12 + p, sibling)
+
+        def forward(p):
+            done(by_links(p))
+            to_sibling(p).start()
+
+        def compute(p, with_near):
+            def item(i, carry):
+                w = p * 8 + i
+                _, origin, y = from_first(load(near_s[w, NEAR_AT]))
+                if with_near:
+                    a = near_item(load, [near_s[w, NEAR_AT + k] for k in range(4)])
+                else:
+                    a = pairs[w]
+                a = a + far_item(cells[w], origin, y)
+                for c in range(3):
+                    force[core, chip, c, pl.ds(w, 1), :] = a[c : c + 1]
+                return carry
+
+            lax.fori_loop(0, 8, item, 0, unroll=4)
+
+        def piece(p, carry, with_near):
+            compute(p, with_near)
+            for c in by_links(p):
+                c.start()
+
+            @pl.when(p > 0)
+            def _():
+                forward(p - 1)
+
             return carry
 
-        cuts, flights = (0, 24, ITEMS), []
-        for begin, end in zip(cuts, cuts[1:]):
-            lax.fori_loop(begin, end, item, 0, unroll=4)
-            flights.append(send(force.at[core, chip, :, pl.ds(begin, end - begin), :], along))
-        last = []
-        for (begin, end), flight in zip(zip(cuts, cuts[1:]), flights):
-            done(flight)
-            last += send(force.at[core, :, :, pl.ds(begin, end - begin), :], [sibling])
-        done(last)
-
-    moments(dense, top_row[...], table_1.at[core, chip, g])
+        if known:
+            lax.fori_loop(0, known // 8, functools.partial(piece, with_near=False), 0)
+        lax.fori_loop(known // 8, 4, functools.partial(piece, with_near=True), 0)
+        compute(4, True)
+        final = send(force.at[core, chip, :, pl.ds(32, 8), :], within)
+        forward(3)
+        done(final)
+        for p in range(4):
+            to_sibling(p).wait()
+
+    moments(dense, top_row[...].astype(f32), table_1.at[core, chip, g])
     flight = send(table_1.at[core, chip, g], across)
     done(list_copies)
     list_copies = send(lists.at[core], [sibling])
     done(flight)
     flight = send(table_1.at[core, chip], along)
+    x_2 = ring_2(x, x_1)
     done(list_copies)
 
     def take(w, carry):
@@ -452,7 +506,6 @@
     lax.fori_loop(0, ITEMS // 4, place, 0)
     for i in range(ITEMS // 8):
         tops[i : i + 1, :] = jnp.concatenate([wanted[8 * i + u : 8 * i + u + 1, 64:96] for u in range(8)], axis=1)
-    x_2 = ring_2(x, x_1)
     for c in to_scalars:
         c.wait()
     number = row_iota((SUB, 128)) * 128 + lax.broadcasted_iota(i32, (SUB, 128), 1)
@@ -468,27 +521,24 @@
 
     done(flight)
     flight = send(table_1.at[core], [sibling])
-    x_3 = ring_3(x, x_1, x_2)
     done(flight)
     top_sums(table_1, part_1)
     flight = send(part_1.at[g], across)
+    x_3 = ring_3(x, x_1, x_2)
     essential_cells(table_1)
+    done(flight)
+    four_parts(top_1, part_1)
+    flight = send(top_1.at[s], within)
     done(x_3)
     ahead_1 = ring_1(ahead)
     done(flight)
-    four_parts(top_1, part_1)
-    flight = send(top_1.at[s], within)
+    top_cells(top_1)
 
     def load_1(n):
         return x[(n >> 7) & 1, n >> 8, n & 127]
 
-    near_part(load_1, 0, 24)
+    finish(load_1, force_1, 0)
     ahead_2 = ring_2(ahead, ahead_1)
-    near_part(load_1, 24, ITEMS)
-    done(flight)
-    top_cells(top_1)
-    ahead_3 = ring_3(ahead, ahead_1, ahead_2)
-    far_and_return(load_1, force_1)
     slot_copy.wait()
 
     def second(b, carry):
@@ -503,8 +553,9 @@
         return carry
 
     lax.fori_loop(0, BUCKETS, second, 0, unroll=4)
-    moments(dense, top_row[...], table_2.at[core, chip, g])
+    moments(dense, top_row[...].astype(f32), table_2.at[core, chip, g])
     flight = send(table_2.at[core, chip, g], across)
+    ahead_3 = ring_3(ahead, ahead_1, ahead_2)
     done(ahead_3)
 
     def load_2(n):
@@ -513,24 +564,24 @@
         moved = p[0:3] + (2.0 * kick * time_step) * p[3:4] * forced(force_1, slot_s[n >> 7, n & 127])
         return jnp.concatenate([moved, x[at][3:4]], axis=0)
 
-    near_part(load_2, 0, 8)
+    near_part(load_2, 0, 4)
     done(flight)
     flight = send(table_2.at[core, chip], along)
-    near_part(load_2, 8, 24)
+    near_part(load_2, 4, 16)
     done(flight)
     flight = send(table_2.at[core], [sibling])
-    near_part(load_2, 24, 32)
+    near_part(load_2, 16, 20)
     done(flight)
     top_sums(table_2, part_2)
     flight = send(part_2.at[g], across)
-    near_part(load_2, 32, ITEMS)
+    essential_cells(table_2)
     done(flight)
     four_parts(top_2, part_2)
     flight = send(top_2.at[s], within)
-    essential_cells(table_2)
+    near_part(load_2, 20, 24)
     done(flight)
     top_cells(top_2)
-    far_and_return(load_2, force_2)
+    finish(load_2, force_2, 24)
 
     def last(b, carry):
         sl = pl.ds(pl.multiple_of(b * WIDE, WIDE), WIDE)
@@ -540,18 +591,8 @@
     lax.fori_loop(0, BUCKETS, last, 0, unroll=4)
 
 
-def by_core(s):
-    return (s & 1) * (SUB // 2) + (s >> 1)
-
-
 def body(positions, velocities, masses, accel_prev, active, bucket_top, near_list, cell_list, top_list, essential, work):
     n = positions.shape[1]
-    wanted = essential.reshape(DOM, -1)
-    codes = (by_core(wanted >> 7) * DOM + jnp.arange(DOM, dtype=i32)[:, None]) * 128 + (wanted & 127)
-    lists = jnp.concatenate([cell_list, top_list, near_list, jnp.zeros((BUCKETS, 28), i32)], axis=1)
-    tail = jnp.concatenate([work, jnp.full((128 - ITEMS,), -1, i32)])[None]
-    packed = jnp.concatenate([lists, codes.reshape(4, 128), tail, jnp.zeros((3, 128), i32)], axis=0)
-
     vm, dma = pltpu.VMEM, pltpu.SemaphoreType.DMA
     flat = vm((3, n), f32)
     group = vm((2, SUB // 2, BUCKETS, 4, WIDE), f32)
@@ -574,13 +615,14 @@
     return pl.pallas_call(
         kernel,
         out_shape=(shape, shape),
-        in_specs=[place(pltpu.SMEM)] + [place(pltpu.HBM)] * 5 + [place(pltpu.VMEM)] * 2,
+        in_specs=[place(pltpu.SMEM)] + [place(pltpu.HBM)] * 5 + [place(pltpu.VMEM)] * 6,
         out_specs=(place(pltpu.VMEM), place(pltpu.VMEM)),
         scratch_shapes=scratch,
-        compiler_params=pltpu.CompilerParams(collective_id=1, has_side_effects=True, vmem_limit_bytes=50 * MIB),
+        compiler_params=pltpu.CompilerParams(collective_id=1, has_side_effects=True, vmem_limit_bytes=62 * MIB),
     )(
         work, positions, velocities, accel_prev, active.reshape(1, n), masses.reshape(1, n),
-        bucket_top.astype(f32).reshape(1, BUCKETS), packed,
+        bucket_top.reshape(1, BUCKETS), cell_list.T, top_list.T, near_list.T, essential.reshape(DOM, -1),
+        work.reshape(1, ITEMS),
     )
 
 

time: 162 us -> 153 us (0.944)
  local copies, waits for them, and re-layouts: 8.83 us -> 2.78 us
    unnamed x17 -> x4, local copies, waits for them, and re-layouts: 7.77 us -> 2.78 us
where the time goes in v4:
time: 153 us
  Pallas kernels  150 us (98%)
  local copies, waits for them, and re-layouts  2.78 us (2%)
    pallas_call x1, Pallas kernels, body(): pl.pallas_call(kernel, out_shape=(shape, shape), in_specs=[place(pltpu.SM...  150 us

profile of v4, /device:TPU:1, one launch (start us, length us, event | category | flops | bytes accessed | tf_op | source)
XLA Modules:
  0.0 153.2 jit_solution(10617894405905952299)
XLA Ops:
  0.6 149.8 %shard_map.122 = (f32[3,32768]{1,0:T(4,128)}, f32[3,32768]{1,0:T(4,128)}) custom-call(s32[40]{0:T(128)} %work.1, f32[3,32768]{1,0:T(4,128)} %pos_in.1, f32[3,32768]{1,0:T(4,128)} %vel_in.1, f32[3,32768]{1,0:T(4,128)} %acc_in.1, s32[1,32768]{1,0:T(1,128)} %bitcast.8, f32[1,32768]{1,0:T(1,128)} %bitcast.9, s32[1,128]{1,0:T(1,128)} %bitcast.15, ...), custom_call_target="tpu_custom_call" | custom-call | tf_op jit(solution)/shard_map/pallas_call | solution.py:615
  150.4 0.0 copy-start
  150.5 2.0 %copy.15 = f32[3,32768]{1,0:T(4,128)} copy(f32[3,32768]{1,0:T(4,128)} %get-tuple-element.4) | data formatting | bytes 786432
  152.4 0.0 copy-done
  152.4 0.8 copy.16
Async XLA Ops:
  150.4 2.0 %copy-start = (f32[3,32768]{1,0:T(4,128)S(1)}, f32[3,32768]{1,0:T(4,128)}, u32[]{:S(2)}) copy-start(f32[3,32768]{1,0:T(4,128)} %get-tuple-element.5) | copy-start | bytes 1179652

commit v5 on v4

--- a/solution.py
+++ b/solution.py
@@ -248,8 +248,7 @@
 
 def forced(force, slot):
     k = jnp.maximum(slot, 0)
-    block, w = k // ITEMS, lax.rem(k, ITEMS)
-    rows = [force[block // 4, lax.rem(block, 4), c, pl.ds(w, 1), :] for c in range(3)]
+    rows = [force[k >> 8, (k >> 6) & 3, c, pl.ds(k & 63, 1), :] for c in range(3)]
     return jnp.where(slot >= 0, jnp.concatenate(rows, axis=0), 0.0)
 
 
@@ -367,8 +366,8 @@
         sums[...] = jnp.zeros_like(sums)
 
         def step(i, carry):
-            at, k = i // 4, (i % 4) * 4
-            got = [top_values(table[at // 4, at % 4, k + u], ids) for u in range(4)]
+            at, k = i >> 2, (i & 3) * 4
+            got = [top_values(table[at >> 2, at & 3, k + u], ids) for u in range(4)]
             v = jnp.concatenate([a for a, _ in got], axis=1)
             o = jnp.concatenate([b for _, b in got], axis=1)
             sums[...] += dot(v, o, (1, 1))
@@ -385,7 +384,7 @@
             top[s, k] = part[4 * k] + part[4 * k + 1] + part[4 * k + 2] + part[4 * k + 3]
 
     def essential_cells(table):
-        spread(lambda k: table[k // 64, k // 16 % 4, k % 16], pieces, SUB * DOM)
+        spread(lambda k: table[k >> 6, (k >> 4) & 3, k & 15], pieces, SUB * DOM)
 
         def gather(i, carry):
             ess = lookup(pieces, SUB * DOM, row[pl.ds(i, 1), :], lane[pl.ds(i, 1), :])
@@ -394,10 +393,10 @@
                 cells[i * 4 + u] = jnp.concatenate([ess[:, u * 64 : u * 64 + 64], blank], axis=1)
             return carry
 
-        lax.fori_loop(0, ITEMS // 4, gather, 0)
+        lax.fori_loop(0, ITEMS // 4, gather, 0, unroll=2)
 
     def top_cells(top):
-        spread(lambda k: top[k // 4, k % 4], top_pieces, 32)
+        spread(lambda k: top[k >> 2, k & 3], top_pieces, 32)
 
         def gather(i, carry):
             t = tops[pl.ds(i, 1), :]
@@ -407,9 +406,9 @@
                 cells[i * 8 + u] += jnp.concatenate([blank[0], far[:, u * 32 : u * 32 + 32], blank[1]], axis=1)
             return carry
 
-        lax.fori_loop(0, ITEMS // 8, gather, 0)
-
-    def finish(load, force, known):
+        lax.fori_loop(0, ITEMS // 8, gather, 0, unroll=5)
+
+    def finish(load, force, known, between=None):
         first_sem = used[0]
         used[0] += 16
 
@@ -461,20 +460,24 @@
 
         if known:
             lax.fori_loop(0, known // 8, functools.partial(piece, with_near=False), 0)
-        lax.fori_loop(known // 8, 4, functools.partial(piece, with_near=True), 0)
+        if known < 24:
+            lax.fori_loop(known // 8, 3, functools.partial(piece, with_near=True), 0)
+        middle = between() if between else None
+        lax.fori_loop(3, 4, functools.partial(piece, with_near=True), 0)
         compute(4, True)
         final = send(force.at[core, chip, :, pl.ds(32, 8), :], within)
         forward(3)
         done(final)
         for p in range(4):
             to_sibling(p).wait()
+        return middle
 
     moments(dense, top_row[...].astype(f32), table_1.at[core, chip, g])
-    flight = send(table_1.at[core, chip, g], across)
+    flight = send(table_1.at[core, chip, g], along)
+    done(flight)
+    flight = send(table_1.at[core, :, g], across)
     done(list_copies)
     list_copies = send(lists.at[core], [sibling])
-    done(flight)
-    flight = send(table_1.at[core, chip], along)
     x_2 = ring_2(x, x_1)
     done(list_copies)
 
@@ -503,7 +506,7 @@
             where[pl.ds(i, 1), :] = jnp.sum(jnp.where(at, found, 0.0), axis=0, keepdims=True).astype(i32)
         return carry
 
-    lax.fori_loop(0, ITEMS // 4, place, 0)
+    lax.fori_loop(0, ITEMS // 4, place, 0, unroll=5)
     for i in range(ITEMS // 8):
         tops[i : i + 1, :] = jnp.concatenate([wanted[8 * i + u : 8 * i + u + 1, 64:96] for u in range(8)], axis=1)
     for c in to_scalars:
@@ -512,34 +515,34 @@
 
     def find(w, found):
         for k in range(SUB):
-            found = jnp.where(number == work_s[k, 4, w], k * ITEMS + w, found)
+            found = jnp.where(number == work_s[k, 4, w], k * 64 + w, found)
         return found
 
-    slots[...] = lax.fori_loop(0, ITEMS, find, jnp.full((SUB, 128), -1, i32))
+    slots[...] = lax.fori_loop(0, ITEMS, find, jnp.full((SUB, 128), -1, i32), unroll=4)
     slot_copy = pltpu.make_async_copy(slots, slot_s, local_sem.at[9])
     slot_copy.start()
 
     done(flight)
     flight = send(table_1.at[core], [sibling])
+    x_3 = ring_3(x, x_1, x_2)
     done(flight)
     top_sums(table_1, part_1)
     flight = send(part_1.at[g], across)
-    x_3 = ring_3(x, x_1, x_2)
     essential_cells(table_1)
     done(flight)
     four_parts(top_1, part_1)
     flight = send(top_1.at[s], within)
     done(x_3)
     ahead_1 = ring_1(ahead)
-    done(flight)
-    top_cells(top_1)
+    slot_copy.wait()
 
     def load_1(n):
         return x[(n >> 7) & 1, n >> 8, n & 127]
 
-    finish(load_1, force_1, 0)
-    ahead_2 = ring_2(ahead, ahead_1)
-    slot_copy.wait()
+    near_part(load_1, 0, 8)
+    done(flight)
+    top_cells(top_1)
+    ahead_2 = finish(load_1, force_1, 8, lambda: ring_2(ahead, ahead_1))
 
     def second(b, carry):
         sl = pl.ds(pl.multiple_of(b * WIDE, WIDE), WIDE)
@@ -554,8 +557,10 @@
 
     lax.fori_loop(0, BUCKETS, second, 0, unroll=4)
     moments(dense, top_row[...].astype(f32), table_2.at[core, chip, g])
-    flight = send(table_2.at[core, chip, g], across)
+    flight = send(table_2.at[core, chip, g], along)
     ahead_3 = ring_3(ahead, ahead_1, ahead_2)
+    done(flight)
+    flight = send(table_2.at[core, :, g], across)
     done(ahead_3)
 
     def load_2(n):
@@ -564,13 +569,10 @@
         moved = p[0:3] + (2.0 * kick * time_step) * p[3:4] * forced(force_1, slot_s[n >> 7, n & 127])
         return jnp.concatenate([moved, x[at][3:4]], axis=0)
 
-    near_part(load_2, 0, 4)
-    done(flight)
-    flight = send(table_2.at[core, chip], along)
-    near_part(load_2, 4, 16)
+    near_part(load_2, 0, 12)
     done(flight)
     flight = send(table_2.at[core], [sibling])
-    near_part(load_2, 16, 20)
+    near_part(load_2, 12, 20)
     done(flight)
     top_sums(table_2, part_2)
     flight = send(part_2.at[g], across)

time: 153 us -> 143 us (0.935)
  Pallas kernels: 150 us -> 139 us
    pallas_call x1, Pallas kernels: 150 us -> 139 us  [body(): pl.pallas_call(kernel, out_shape=(shape, shape), in_specs=[place(pltpu.SM...]
where the time goes in v5:
time: 143 us; the launch traced here: 142 us
  Pallas kernels  139 us (97%)
  local copies, waits for them, and re-layouts  2.78 us (2%)
    pallas_call x1, Pallas kernels, body(): pl.pallas_call(kernel, out_shape=(shape, shape), in_specs=[place(pltpu.SM...  139 us

profile of v5, /device:TPU:1, one launch (start us, length us, event | category | flops | bytes accessed | tf_op | source)
XLA Modules:
  0.0 142.3 jit_solution(2073453748853158271)
XLA Ops:
  0.6 138.9 %shard_map.122 = (f32[3,32768]{1,0:T(4,128)}, f32[3,32768]{1,0:T(4,128)}) custom-call(s32[40]{0:T(128)} %work.1, f32[3,32768]{1,0:T(4,128)} %pos_in.1, f32[3,32768]{1,0:T(4,128)} %vel_in.1, f32[3,32768]{1,0:T(4,128)} %acc_in.1, s32[1,32768]{1,0:T(1,128)} %bitcast.8, f32[1,32768]{1,0:T(1,128)} %bitcast.9, s32[1,128]{1,0:T(1,128)} %bitcast.15, ...), custom_call_target="tpu_custom_call" | custom-call | tf_op jit(solution)/shard_map/pallas_call | solution.py:617
  139.5 0.0 copy-start
  139.5 2.0 %copy.15 = f32[3,32768]{1,0:T(4,128)} copy(f32[3,32768]{1,0:T(4,128)} %get-tuple-element.4) | data formatting | bytes 786432
  141.5 0.0 copy-done
  141.5 0.8 copy.16
Async XLA Ops:
  139.5 2.0 %copy-start = (f32[3,32768]{1,0:T(4,128)S(1)}, f32[3,32768]{1,0:T(4,128)}, u32[]{:S(2)}) copy-start(f32[3,32768]{1,0:T(4,128)} %get-tuple-element.5) | copy-start | bytes 1179652

commit v6 on v5

--- a/solution.py
+++ b/solution.py
@@ -62,13 +62,12 @@
     first = [dense[c][:, 0:1] for c in range(3)]
     y = [dense[c] - first[c] for c in range(3)]
     m = dense[3]
-    ones = jnp.ones((8, WIDE), f32)
-    lead = jnp.where(lax.broadcasted_iota(i32, (8, WIDE), 1) == 0, 1.0, 0.0)
+    ones = jnp.ones((16, WIDE), f32)
+    lead = jnp.where(lax.broadcasted_iota(i32, (16, WIDE), 1) == 0, 1.0, 0.0)
 
     def total(a, by=ones):
-        return lax.dot_general(
-            by, a, (((1,), (1,)), ((), ())), precision=lax.Precision.HIGHEST, preferred_element_type=f32
-        )[0:1]
+        h, m, l = split3(a)
+        return (dot(by, h, (1, 1)) + (dot(by, m, (1, 1)) + dot(by, l, (1, 1))))[0:1]
 
     my = [m * y[c] for c in range(3)]
     mass = total(m)
@@ -188,11 +187,11 @@
     ch, cm, cl = split3(c)
     fh, fm, fl = split3(phi)
     sq = dot(
+        jnp.concatenate([fh, fm, fh, fm, fl, fh], axis=0),
         jnp.concatenate([ch, ch, cm, cm, ch, cl], axis=0),
-        jnp.concatenate([fh, fm, fh, fm, fl, fh], axis=0),
         (0, 0),
     )
-    s, q = sq[0:128], sq[128:256]
+    s, q = sq[:, 0:128], sq[:, 128:256]
     r = lax.rsqrt(s)
     r2 = r * r
     r3 = r * r2
@@ -200,15 +199,16 @@
     l1 = pick({0: mass * px, 1: mass * py, 2: mass * pz, 3: -mass}, (16, 128))
     l2 = pick({0: 2.5 * px, 1: 2.5 * py, 2: 2.5 * pz, 3: -2.5 * one}, (16, 128))
     l3 = pick({0: -gx, 1: -gy, 2: -gz, 4: qxx, 5: qyy, 6: qzz, 7: qxy, 8: qxz, 9: qyz}, (16, 128))
-    out = jnp.zeros((32, WIDE), f32)
+    out = jnp.zeros((WIDE, 32), f32)
     for l, v in ((l1, r3), (l2, q * (r5 * r2)), (l3, r5)):
         lh = rnd(l)
         pieces = jnp.concatenate([lh, rnd(l - lh)], axis=0)
         vh = v.astype(bf16)
         vm = (v - vh.astype(f32)).astype(bf16)
         out = out + dot(
-            jnp.concatenate([pieces, pieces], axis=1), jnp.concatenate([vh, vm], axis=0), (1, 0)
+            jnp.concatenate([vh, vm], axis=1), jnp.concatenate([pieces, pieces], axis=1), (1, 1)
         )
+    out = out.T
     t = out[0:16] + out[16:32]
     axx, ayy, azz, axy, axz, ayz = [t[i : i + 1] for i in range(4, 10)]
     turned = pick(
@@ -333,17 +333,23 @@
         h = vel[:, sl] + kick * a * acc[:, sl]
         p = pos[:, sl] + time_step * h
         half[:, sl] = h
-        m = mass[:, sl]
-        x[core, chip, b] = jnp.concatenate([p, m], axis=0)
-        ahead[core, chip, b] = jnp.concatenate([p + time_step * h, a], axis=0)
-        for c in range(3):
-            dense[c, pl.ds(b, 1), :] = p[c : c + 1]
-        dense[3, pl.ds(b, 1), :] = m
+        x[core, chip, b] = jnp.concatenate([p, mass[:, sl]], axis=0)
         return carry
 
-    lax.fori_loop(0, BUCKETS, first, 0, unroll=4)
+    lax.fori_loop(0, BUCKETS, first, 0, unroll=8)
     pl.semaphore_wait(barrier, DOM + SUB - 2)
     x_1 = ring_1(x)
+
+    def onward(b, carry):
+        sl = pl.ds(pl.multiple_of(b * WIDE, WIDE), WIDE)
+        p = x[core, chip, b]
+        next_p = p[0:3] + time_step * half[:, sl]
+        ahead[core, chip, b] = jnp.concatenate([next_p, act[:, sl].astype(f32)], axis=0)
+        for c in range(4):
+            dense[c, pl.ds(b, 1), :] = p[c : c + 1]
+        return carry
+
+    lax.fori_loop(0, BUCKETS, onward, 0, unroll=8)
     turned = [cell_list[...], top_list[...], near_list[...], jnp.zeros((28, BUCKETS), i32)]
     lists[core, chip, 0:BUCKETS, :] = jnp.concatenate(turned, axis=0).T
     asked = requests[...]
@@ -479,6 +485,8 @@
     done(list_copies)
     list_copies = send(lists.at[core], [sibling])
     x_2 = ring_2(x, x_1)
+    done(flight)
+    flight = send(table_1.at[core], [sibling])
     done(list_copies)
 
     def take(w, carry):
@@ -523,11 +531,9 @@
     slot_copy.start()
 
     done(flight)
-    flight = send(table_1.at[core], [sibling])
-    x_3 = ring_3(x, x_1, x_2)
-    done(flight)
     top_sums(table_1, part_1)
     flight = send(part_1.at[g], across)
+    x_3 = ring_3(x, x_1, x_2)
     essential_cells(table_1)
     done(flight)
     four_parts(top_1, part_1)

time: 143 us -> 142 us (level)
  no operation moved by 1% of the time
where the time goes in v6:
time: 142 us
  Pallas kernels  138 us (97%)
  local copies, waits for them, and re-layouts  2.78 us (2%)
    pallas_call x1, Pallas kernels, body(): pl.pallas_call(kernel, out_shape=(shape, shape), in_specs=[place(pltpu.SM...  138 us

profile of v6, /device:TPU:1, one launch (start us, length us, event | category | flops | bytes accessed | tf_op | source)
XLA Modules:
  0.0 141.6 jit_solution(1199488308226900271)
XLA Ops:
  0.6 138.2 %shard_map.122 = (f32[3,32768]{1,0:T(4,128)}, f32[3,32768]{1,0:T(4,128)}) custom-call(s32[40]{0:T(128)} %work.1, f32[3,32768]{1,0:T(4,128)} %pos_in.1, f32[3,32768]{1,0:T(4,128)} %vel_in.1, f32[3,32768]{1,0:T(4,128)} %acc_in.1, s32[1,32768]{1,0:T(1,128)} %bitcast.8, f32[1,32768]{1,0:T(1,128)} %bitcast.9, s32[1,128]{1,0:T(1,128)} %bitcast.15, ...), custom_call_target="tpu_custom_call" | custom-call | tf_op jit(solution)/shard_map/pallas_call | solution.py:623
  138.9 0.0 copy-start
  138.9 2.0 %copy.15 = f32[3,32768]{1,0:T(4,128)} copy(f32[3,32768]{1,0:T(4,128)} %get-tuple-element.4) | data formatting | bytes 786432
  140.8 0.0 copy-done
  140.8 0.8 copy.16
Async XLA Ops:
  138.9 2.0 %copy-start = (f32[3,32768]{1,0:T(4,128)S(1)}, f32[3,32768]{1,0:T(4,128)}, u32[]{:S(2)}) copy-start(f32[3,32768]{1,0:T(4,128)} %get-tuple-element.5) | copy-start | bytes 1179652

commit v7 on v6

--- a/solution.py
+++ b/solution.py
@@ -458,10 +458,6 @@
             for c in by_links(p):
                 c.start()
 
-            @pl.when(p > 0)
-            def _():
-                forward(p - 1)
-
             return carry
 
         if known:
@@ -472,7 +468,8 @@
         lax.fori_loop(3, 4, functools.partial(piece, with_near=True), 0)
         compute(4, True)
         final = send(force.at[core, chip, :, pl.ds(32, 8), :], within)
-        forward(3)
+        for p in range(4):
+            forward(p)
         done(final)
         for p in range(4):
             to_sibling(p).wait()

time: 142 us -> 137 us (0.965)
  Pallas kernels: 138 us -> 133 us
    pallas_call x1, Pallas kernels: 138 us -> 133 us  [body(): pl.pallas_call(kernel, out_shape=(shape, shape), in_specs=[place(pltpu.SM...]
where the time goes in v7:
time: 137 us
  Pallas kernels  133 us (97%)
  local copies, waits for them, and re-layouts  2.78 us (2%)
    pallas_call x1, Pallas kernels, body(): pl.pallas_call(kernel, out_shape=(shape, shape), in_specs=[place(pltpu.SM...  133 us
    unnamed x4, local copies, waits for them, and re-layouts  2.78 us

profile of v7, /device:TPU:1, one launch (start us, length us, event | category | flops | bytes accessed | tf_op | source)
XLA Modules:
  0.0 136.6 jit_solution(3570465880027582356)
XLA Ops:
  0.6 133.2 %shard_map.122 = (f32[3,32768]{1,0:T(4,128)}, f32[3,32768]{1,0:T(4,128)}) custom-call(s32[40]{0:T(128)} %work.1, f32[3,32768]{1,0:T(4,128)} %pos_in.1, f32[3,32768]{1,0:T(4,128)} %vel_in.1, f32[3,32768]{1,0:T(4,128)} %acc_in.1, s32[1,32768]{1,0:T(1,128)} %bitcast.8, f32[1,32768]{1,0:T(1,128)} %bitcast.9, s32[1,128]{1,0:T(1,128)} %bitcast.15, ...), custom_call_target="tpu_custom_call" | custom-call | tf_op jit(solution)/shard_map/pallas_call | solution.py:620
  133.8 0.0 copy-start
  133.8 2.0 %copy.15 = f32[3,32768]{1,0:T(4,128)} copy(f32[3,32768]{1,0:T(4,128)} %get-tuple-element.4) | data formatting | bytes 786432
  135.8 0.0 copy-done
  135.8 0.8 copy.16
Async XLA Ops:
  133.8 2.0 %copy-start = (f32[3,32768]{1,0:T(4,128)S(1)}, f32[3,32768]{1,0:T(4,128)}, u32[]{:S(2)}) copy-start(f32[3,32768]{1,0:T(4,128)} %get-tuple-element.5) | copy-start | bytes 1179652
